TPU v7x, 512 devices: a whole 4x4x16 slice. The times are simulated.
512 devices in a mesh: gx: 32 (over z, y_hi), gy: 16 (over y_lo, x, core).
Axes of the slice: x: 4, y: 4 (y_hi: 2, y_lo: 2; y = y_hi * 2 + y_lo), z: 16, core: 2. Of those that a mesh axis runs over, the one named last changes fastest.
Arguments:
- velocity: float32 [2, 20, 256, 2048], P(None, None, 'gx', 'gy'), may hold values from -6 to 6
- drive: float32 [2, 256, 2048], P(None, 'gx', 'gy'), may hold values from -0.6 to 0.6
- stiffness: float32 [256, 2048], P('gx', 'gy'), may hold values from 0.5 to 2
- thickness: float32 [256, 2048], P('gx', 'gy'), may hold values from 0.5 to 2
- ice_mask: int32 [256, 2048], P('gx', 'gy'), may hold values from 0 to 1
- friction_class: int32 [256, 2048], P('gx', 'gy'), may hold values from 0 to 7
- friction_table: float32 [8], replicated, may hold values from 0.1 to 10
Outputs:
- velocity_out: float32 [2, 20, 256, 2048], P(None, None, 'gx', 'gy')
- residual: float32 [2, 20, 256, 2048], P(None, None, 'gx', 'gy')
All inputs are finite; a program needn't handle non-finite values.
Results may differ from a plain program's by a relative error of at most 0.0003.
Values sent between devices are 32-bit elements; how exact they have to be, the bound alone decides.
No kernel may reach another device: no remote copies, remote signals or barrier semaphores. Data moves between devices by JAX's collectives and lax.ppermute only.
A program may use at most 128 MiB of HBM per device.

v0:
```python
import jax
import jax.numpy as jnp
from jax import lax
from jax.sharding import PartitionSpec as P

PRE = 2
POST = 2
COARSE = 4


OMEGA = 0.8
EPS0 = 0.01
FACTOR_X = (4.0, 1.0)
FACTOR_Y = (1.0, 4.0)


def extended(cells, sides, width):
    for axis, dim in sides:
        count = lax.axis_size(axis)
        ends = count - 1
        head = lax.slice_in_dim(cells, 0, width, axis=dim)
        tail = lax.slice_in_dim(cells, cells.shape[dim] - width, cells.shape[dim], axis=dim)
        cells = jnp.concatenate(
            [
                lax.ppermute(tail, axis, [(i, (i + 1) % count) for i in range(ends)]),
                cells,
                lax.ppermute(head, axis, [((i + 1) % count, i) for i in range(ends)]),
            ],
            axis=dim,
        )
    return cells


def viscosity(padded, stiffness, thickness):
    layers = padded.shape[1]
    spacing = thickness / layers
    centre = padded[:, :, 1:-1, 1:-1]
    slope_first = (padded[:, :, 2:, 1:-1] - padded[:, :, :-2, 1:-1]) * 0.5
    slope_second = (padded[:, :, 1:-1, 2:] - padded[:, :, 1:-1, :-2]) * 0.5
    upper_cells = jnp.concatenate([centre[:, 1:], centre[:, -1:]], axis=1)
    lower_cells = jnp.concatenate([centre[:, :1], centre[:, :-1]], axis=1)
    slope_vert = (upper_cells - lower_cells) / (2.0 * spacing)
    shear_sum = slope_second[0] + slope_first[1]
    strain_rate = (
        slope_first[0] * slope_first[0]
        + slope_second[1] * slope_second[1]
        + slope_first[0] * slope_second[1]
        + 0.25 * shear_sum * shear_sum
        + 0.25 * (slope_vert[0] * slope_vert[0] + slope_vert[1] * slope_vert[1])
        + EPS0
    )
    return 0.5 * stiffness * strain_rate ** (-1.0 / 3.0)


def build_operator(padded_eta, ice_float, bed_drag, thickness, scale):
    centre = padded_eta[:, 1:-1, 1:-1]
    east_face = scale * jnp.sqrt(centre * padded_eta[:, 2:, 1:-1])
    west_face = scale * jnp.sqrt(centre * padded_eta[:, :-2, 1:-1])
    north_face = scale * jnp.sqrt(centre * padded_eta[:, 1:-1, 2:])
    south_face = scale * jnp.sqrt(centre * padded_eta[:, 1:-1, :-2])
    layers = centre.shape[0]
    spacing = thickness / layers
    vert_faces = 0.5 * (centre[1:] + centre[:-1]) / (spacing * spacing)
    zero_row = jnp.zeros_like(centre[:1])
    upper_face = jnp.concatenate([vert_faces, zero_row], axis=0)
    lower_face = jnp.concatenate([zero_row, vert_faces], axis=0)
    bed_row = jnp.concatenate([(bed_drag / spacing)[None], jnp.zeros_like(centre[1:])], axis=0)
    common = upper_face + lower_face + bed_row + (1.0 - ice_float)
    diagonal = jnp.stack(
        [
            FACTOR_X[component] * (east_face + west_face)
            + FACTOR_Y[component] * (north_face + south_face)
            + common
            for component in range(2)
        ]
    )
    return (east_face, west_face, north_face, south_face, upper_face, lower_face, diagonal)


def apply_operator(coeffs, padded):
    east_face, west_face, north_face, south_face, upper_face, lower_face, diagonal = coeffs
    centre = padded[:, :, 1:-1, 1:-1]
    zero_row = jnp.zeros_like(centre[:, :1])
    upper_cells = jnp.concatenate([centre[:, 1:], zero_row], axis=1)
    lower_cells = jnp.concatenate([zero_row, centre[:, :-1]], axis=1)
    result = []
    for component in range(2):
        across = (
            east_face * padded[component, :, 2:, 1:-1] + west_face * padded[component, :, :-2, 1:-1]
        )
        sideways = (
            north_face * padded[component, :, 1:-1, 2:]
            + south_face * padded[component, :, 1:-1, :-2]
        )
        vertical = upper_face * upper_cells[component] + lower_face * lower_cells[component]
        result.append(
            diagonal[component] * centre[component]
            - FACTOR_X[component] * across
            - FACTOR_Y[component] * sideways
            - vertical
        )
    return jnp.stack(result)


def column_solve(coeffs, forcing):
    upper_face, lower_face, diagonal = (coeffs[4], coeffs[5], coeffs[6])
    layers = forcing.shape[1]
    ratios = []
    partials = []
    for layer in range(layers):
        if layer == 0:
            pivot_value = diagonal[:, 0]
            partial_value = forcing[:, 0] / pivot_value
        else:
            pivot_value = diagonal[:, layer] - lower_face[layer] * ratios[-1]
            partial_value = (forcing[:, layer] + lower_face[layer] * partials[-1]) / pivot_value
        ratios.append(upper_face[layer] / pivot_value)
        partials.append(partial_value)
    solved = [partials[-1]]
    for layer in range(layers - 2, -1, -1):
        solved.append(partials[layer] + ratios[layer] * solved[-1])
    return jnp.stack(solved[::-1], axis=1)


def smooth_sweep(coeffs, forcing, field, extend):
    remainder = forcing - apply_operator(coeffs, extend(field))
    return field + OMEGA * column_solve(coeffs, remainder)


def drag_lookup(friction_class, friction_table):
    classes = jnp.arange(friction_table.shape[0], dtype=jnp.int32)
    matches = (friction_class[None] == classes[:, None, None]).astype(jnp.float32)
    return jnp.sum(matches * friction_table[:, None, None], axis=0)


def block_mean(field):
    sizes_in = field.shape
    grouped = field.reshape(sizes_in[:-2] + (sizes_in[-2] // 2, 2, sizes_in[-1] // 2, 2))
    return jnp.sum(grouped, axis=(-3, -1)) * 0.25


def block_any(field):
    sizes_in = field.shape
    grouped = field.reshape(sizes_in[:-2] + (sizes_in[-2] // 2, 2, sizes_in[-1] // 2, 2))
    return jnp.max(grouped, axis=(-3, -1))


def prolongate(field):
    return jnp.repeat(jnp.repeat(field, 2, axis=-2), 2, axis=-1)


def fine_extend(field):
    return extended(field, (("gx", 2), ("gy", 3)), 1)


def per_device(velocity, drive, stiffness, thickness, ice_mask, friction_class, friction_table):
    ice_float = ice_mask.astype(jnp.float32)
    initial = velocity * ice_float
    bed_drag = ice_float * drag_lookup(friction_class, friction_table)
    padded = extended(initial, (("gx", 2), ("gy", 3)), 1)
    masked = viscosity(padded, stiffness, thickness) * ice_float
    padded_eta = extended(masked, (("gx", 1), ("gy", 2)), 1)
    coeffs = build_operator(padded_eta, ice_float, bed_drag, thickness, 1.0)
    forcing = jnp.broadcast_to((drive * ice_float)[:, None], velocity.shape)
    current = initial
    for turn_index in range(PRE):
        current = smooth_sweep(coeffs, forcing, current, fine_extend)
    remainder = forcing - apply_operator(coeffs, fine_extend(current))
    coarse_mask = block_any(ice_mask).astype(jnp.float32)
    coarse_eta = block_mean(masked)
    coarse_drag = block_mean(bed_drag)
    coarse_thick = block_mean(thickness)
    coarse_forcing = block_mean(remainder)
    eta_rim = extended(coarse_eta, (("gx", 1), ("gy", 2)), 1)
    coarse_coeffs = build_operator(eta_rim, coarse_mask, coarse_drag, coarse_thick, 0.25)

    def coarse_extend(field):
        return extended(field, (("gx", 2), ("gy", 3)), 1)

    correction = jnp.zeros_like(coarse_forcing)
    for turn_index in range(COARSE):
        correction = smooth_sweep(coarse_coeffs, coarse_forcing, correction, coarse_extend)
    current = current + ice_float * prolongate(correction)
    for turn_index in range(POST):
        current = smooth_sweep(coeffs, forcing, current, fine_extend)
    residual = forcing - apply_operator(coeffs, fine_extend(current))
    return (current, residual)


def solution(mesh):
    return jax.shard_map(
        per_device,
        mesh=mesh,
        in_specs=(
            P(None, None, "gx", "gy"),
            P(None, "gx", "gy"),
            P("gx", "gy"),
            P("gx", "gy"),
            P("gx", "gy"),
            P("gx", "gy"),
            P(),
        ),
        out_specs=(P(None, None, "gx", "gy"), P(None, None, "gx", "gy")),
        check_vma=False,
    )
```

profile of v0, /device:TPU:391, one launch (start us, length us, event | category | flops | bytes accessed | tf_op | source)
XLA Modules:
  0.0 302.4 jit_solution(16757858861316694471)
XLA Ops:
  0.7 6.5 %collective-permute-start.20 = (f32[2,20,1,64]{3,2,1,0:T(1,128)S(1)}, f32[2,20,1,64]{3,2,1,0:T(1,128)S(1)}, u32[]{:S(2)}, u32[]{:S(2)}) collective-permute-start(f32[2,20,1,64]{3,2,1,0:T(1,128)S(1)} %broadcast.9299), channel_id=1, source_target_pairs={{16,0},{32,16},{48,32},{64,48},{80,64},{96,80},{112,96},{128,112},... | collective-permute-start | bytes 30728 | tf_op jit(solution)/shard_map/ppermute | solution.py:27
  14.2 4.8 %collective-permute-start = (f32[2,20,1,128]{3,2,1,0:T(1,128)S(1)}, f32[2,20,1,128]{3,2,1,0:T(1,128)S(1)}, u32[]{:S(2)}, u32[]{:S(2)}) collective-permute-start(f32[2,20,1,128]{3,2,1,0:T(1,128)S(1)} %get-tuple-element.367), channel_id=1, source_target_pairs={{16,0},{32,16},{48,32},{64,48},{80,64},{96,80},{112,96},{128,112},... | collective-permute-start | bytes 61448 | tf_op jit(solution)/shard_map/ppermute | solution.py:27
  39.7 6.6 %collective-permute-done.2 = f32[2,20,10,1]{3,2,1,0:T(8,128)S(1)} collective-permute-done((f32[2,20,10,1]{3,2,1,0:T(8,128)S(1)}, f32[2,20,10,1]{3,2,1,0:T(8,128)S(1)}, u32[]{:S(2)}, u32[]{:S(2)}) %collective-permute-start.2) | collective-permute-done | bytes 1632 | tf_op jit(solution)/shard_map/ppermute | solution.py:27
  47.4 4.8 %collective-permute-start.4 = (f32[20,1,128]{2,1,0:T(1,128)}, f32[20,1,128]{2,1,0:T(1,128)S(1)}, u32[]{:S(2)}, u32[]{:S(2)}) collective-permute-start(f32[20,1,128]{2,1,0:T(1,128)} %get-tuple-element.400), channel_id=1, source_target_pairs={{16,0},{32,16},{48,32},{64,48},{80,64},{96,80},{112,96},{128,112},... | collective-permute-start | bytes 30728 | tf_op jit(solution)/shard_map/ppermute | solution.py:27
  63.4 6.0 %collective-permute-start.16 = (f32[20,1,64]{2,1,0:T(1,128)S(1)}, f32[20,1,64]{2,1,0:T(1,128)S(1)}, u32[]{:S(2)}, u32[]{:S(2)}) collective-permute-start(f32[20,1,64]{2,1,0:T(1,128)S(1)} %get-tuple-element.424), channel_id=1, source_target_pairs={{16,0},{32,16},{48,32},{64,48},{80,64},{96,80},{112,96},{128,112},... | collective-permute-start | bytes 15368 | tf_op jit(solution)/shard_map/ppermute | solution.py:27
  72.3 5.8 %collective-permute-start.19 = (f32[20,6,1]{2,0,1:T(8,128)S(1)}, f32[20,6,1]{2,0,1:T(8,128)S(1)}, u32[]{:S(2)}, u32[]{:S(2)}) collective-permute-start(f32[20,6,1]{2,0,1:T(8,128)S(1)} %get-tuple-element.423), channel_id=1, source_target_pairs={{0,1},{1,2},{2,3},{3,4},{4,5},{5,6},{6,7},{7,8},{8,9},{9,10},{10,1... | collective-permute-start | bytes 1448 | tf_op jit(solution)/shard_map/ppermute | solution.py:25
  82.7 6.2 %collective-permute-done.6 = f32[20,10,1]{2,1,0:T(8,128)S(1)} collective-permute-done((f32[20,10,1]{2,1,0:T(8,128)S(1)}, f32[20,10,1]{2,1,0:T(8,128)S(1)}, u32[]{:S(2)}, u32[]{:S(2)}) %collective-permute-start.6) | collective-permute-done | bytes 832 | tf_op jit(solution)/shard_map/ppermute | solution.py:27
  91.6 7.4 %collective-permute-start.8 = (f32[2,20,1,128]{3,2,1,0:T(1,128)S(1)}, f32[2,20,1,128]{3,2,1,0:T(1,128)S(1)}, u32[]{:S(2)}, u32[]{:S(2)}) collective-permute-start(f32[2,20,1,128]{3,2,1,0:T(1,128)S(1)} %get-tuple-element.360), channel_id=1, source_target_pairs={{16,0},{32,16},{48,32},{64,48},{80,64},{96,80},{112,96},{128,112},... | collective-permute-start | bytes 61448 | tf_op jit(solution)/shard_map/ppermute | solution.py:27
  101.2 6.0 %collective-permute-done.9 = f32[2,20,1,128]{3,2,1,0:T(1,128)S(1)} collective-permute-done((f32[2,20,1,128]{3,2,1,0:T(1,128)S(1)}, f32[2,20,1,128]{3,2,1,0:T(1,128)S(1)}, u32[]{:S(2)}, u32[]{:S(2)}) %collective-permute-start.9) | collective-permute-done | bytes 20512 | tf_op jit(solution)/shard_map/ppermute | solution.py:25
  113.8 6.5 %collective-permute-done.10 = f32[2,20,10,1]{3,2,1,0:T(8,128)S(1)} collective-permute-done((f32[2,20,10,1]{3,2,1,0:T(8,128)S(1)}, f32[2,20,10,1]{3,2,1,0:T(8,128)S(1)}, u32[]{:S(2)}, u32[]{:S(2)}) %collective-permute-start.10) | collective-permute-done | bytes 1632 | tf_op jit(solution)/shard_map/ppermute | solution.py:27
  138.6 6.6 %collective-permute-done.14 = f32[2,20,10,1]{3,2,1,0:T(8,128)S(1)} collective-permute-done((f32[2,20,10,1]{3,2,1,0:T(8,128)S(1)}, f32[2,20,10,1]{3,2,1,0:T(8,128)S(1)}, u32[]{:S(2)}, u32[]{:S(2)}) %collective-permute-start.14) | collective-permute-done | bytes 1632 | tf_op jit(solution)/shard_map/ppermute | solution.py:27
  152.4 5.1 %collective-permute-start.24 = (f32[2,20,1,64]{3,2,1,0:T(1,128)S(1)}, f32[2,20,1,64]{3,2,1,0:T(1,128)S(1)}, u32[]{:S(2)}, u32[]{:S(2)}) collective-permute-start(f32[2,20,1,64]{3,2,1,0:T(1,128)S(1)} %get-tuple-element.395), channel_id=1, source_target_pairs={{16,0},{32,16},{48,32},{64,48},{80,64},{96,80},{112,96},{128,112},... | collective-permute-start | bytes 30728 | tf_op jit(solution)/shard_map/ppermute | solution.py:27
  160.6 5.8 %collective-permute-start.27 = (f32[2,20,6,1]{3,0,2,1:T(2,128)S(1)}, f32[2,20,6,1]{3,0,2,1:T(2,128)S(1)}, u32[]{:S(2)}, u32[]{:S(2)}) collective-permute-start(f32[2,20,6,1]{3,0,2,1:T(2,128)S(1)} %get-tuple-element.382), channel_id=1, source_target_pairs={{0,1},{1,2},{2,3},{3,4},{4,5},{5,6},{6,7},{7,8},{8,9},{9,10},{10,1... | collective-permute-start | bytes 2888 | tf_op jit(solution)/shard_map/ppermute | solution.py:25
  173.1 6.3 %collective-permute-start.28 = (f32[2,20,1,64]{3,2,1,0:T(1,128)S(1)}, f32[2,20,1,64]{3,2,1,0:T(1,128)S(1)}, u32[]{:S(2)}, u32[]{:S(2)}) collective-permute-start(f32[2,20,1,64]{3,2,1,0:T(1,128)S(1)} %get-tuple-element.391), channel_id=1, source_target_pairs={{16,0},{32,16},{48,32},{64,48},{80,64},{96,80},{112,96},{128,112},... | collective-permute-start | bytes 30728 | tf_op jit(solution)/shard_map/ppermute | solution.py:27
  182.4 7.3 %collective-permute-start.31 = (f32[2,20,6,1]{3,0,2,1:T(2,128)S(1)}, f32[2,20,6,1]{3,0,2,1:T(2,128)S(1)}, u32[]{:S(2)}, u32[]{:S(2)}) collective-permute-start(f32[2,20,6,1]{3,0,2,1:T(2,128)S(1)} %get-tuple-element.378), channel_id=1, source_target_pairs={{0,1},{1,2},{2,3},{3,4},{4,5},{5,6},{6,7},{7,8},{8,9},{9,10},{10,1... | collective-permute-start | bytes 2888 | tf_op jit(solution)/shard_map/ppermute | solution.py:25
  195.5 7.5 %collective-permute-start.32 = (f32[2,20,1,64]{3,2,1,0:T(1,128)S(1)}, f32[2,20,1,64]{3,2,1,0:T(1,128)S(1)}, u32[]{:S(2)}, u32[]{:S(2)}) collective-permute-start(f32[2,20,1,64]{3,2,1,0:T(1,128)S(1)} %get-tuple-element.387), channel_id=1, source_target_pairs={{16,0},{32,16},{48,32},{64,48},{80,64},{96,80},{112,96},{128,112},... | collective-permute-start | bytes 30728 | tf_op jit(solution)/shard_map/ppermute | solution.py:27
  206.1 6.7 %collective-permute-start.35 = (f32[2,20,6,1]{3,0,2,1:T(2,128)S(1)}, f32[2,20,6,1]{3,0,2,1:T(2,128)S(1)}, u32[]{:S(2)}, u32[]{:S(2)}) collective-permute-start(f32[2,20,6,1]{3,0,2,1:T(2,128)S(1)} %get-tuple-element.374), channel_id=1, source_target_pairs={{0,1},{1,2},{2,3},{3,4},{4,5},{5,6},{6,7},{7,8},{8,9},{9,10},{10,1... | collective-permute-start | bytes 2888 | tf_op jit(solution)/shard_map/ppermute | solution.py:25
  216.9 8.1 %collective-permute-start.36 = (f32[2,20,1,128]{3,2,1,0:T(1,128)S(1)}, f32[2,20,1,128]{3,2,1,0:T(1,128)S(1)}, u32[]{:S(2)}, u32[]{:S(2)}) collective-permute-start(f32[2,20,1,128]{3,2,1,0:T(1,128)S(1)} %get-tuple-element.352), channel_id=1, source_target_pairs={{16,0},{32,16},{48,32},{64,48},{80,64},{96,80},{112,96},{128,112},... | collective-permute-start | bytes 61448 | tf_op jit(solution)/shard_map/ppermute | solution.py:27
  227.0 6.2 %collective-permute-done.37 = f32[2,20,1,128]{3,2,1,0:T(1,128)S(1)} collective-permute-done((f32[2,20,1,128]{3,2,1,0:T(1,128)S(1)}, f32[2,20,1,128]{3,2,1,0:T(1,128)S(1)}, u32[]{:S(2)}, u32[]{:S(2)}) %collective-permute-start.37) | collective-permute-done | bytes 20512 | tf_op jit(solution)/shard_map/ppermute | solution.py:25
  233.4 7.3 %collective-permute-start.39 = (f32[2,20,10,1]{3,2,1,0:T(8,128)S(1)}, f32[2,20,10,1]{3,2,1,0:T(8,128)S(1)}, u32[]{:S(2)}, u32[]{:S(2)}) collective-permute-start(f32[2,20,10,1]{3,2,1,0:T(8,128)S(1)} %get-tuple-element.315), channel_id=1, source_target_pairs={{0,1},{1,2},{2,3},{3,4},{4,5},{5,6},{6,7},{7,8},{8,9},{9,10},{10,1... | collective-permute-start | bytes 4808 | tf_op jit(solution)/shard_map/ppermute | solution.py:25
  244.7 6.5 %collective-permute-done.38 = f32[2,20,10,1]{3,2,1,0:T(8,128)S(1)} collective-permute-done((f32[2,20,10,1]{3,2,1,0:T(8,128)S(1)}, f32[2,20,10,1]{3,2,1,0:T(8,128)S(1)}, u32[]{:S(2)}, u32[]{:S(2)}) %collective-permute-start.38) | collective-permute-done | bytes 1632 | tf_op jit(solution)/shard_map/ppermute | solution.py:27
  254.4 4.6 %collective-permute-start.41 = (f32[2,20,1,128]{3,2,1,0:T(1,128)S(1)}, f32[2,20,1,128]{3,2,1,0:T(1,128)S(1)}, u32[]{:S(2)}, u32[]{:S(2)}) collective-permute-start(f32[2,20,1,128]{3,2,1,0:T(1,128)S(1)} %get-tuple-element.347), channel_id=1, source_target_pairs={{0,16},{16,32},{32,48},{48,64},{64,80},{80,96},{96,112},{112,128},... | collective-permute-start | bytes 61448 | tf_op jit(solution)/shard_map/ppermute | solution.py:25
  269.4 6.5 %collective-permute-done.42 = f32[2,20,10,1]{3,2,1,0:T(8,128)S(1)} collective-permute-done((f32[2,20,10,1]{3,2,1,0:T(8,128)S(1)}, f32[2,20,10,1]{3,2,1,0:T(8,128)S(1)}, u32[]{:S(2)}, u32[]{:S(2)}) %collective-permute-start.42) | collective-permute-done | bytes 1632 | tf_op jit(solution)/shard_map/ppermute | solution.py:27
  294.8 6.5 %collective-permute-done.46 = f32[2,20,10,1]{3,2,1,0:T(8,128)S(1)} collective-permute-done((f32[2,20,10,1]{3,2,1,0:T(8,128)S(1)}, f32[2,20,10,1]{3,2,1,0:T(8,128)S(1)}, u32[]{:S(2)}, u32[]{:S(2)}) %collective-permute-start.46) | collective-permute-done | bytes 1632 | tf_op jit(solution)/shard_map/ppermute | solution.py:27
  (445 shorter events, 147.9 us)
Async XLA Ops:
  0.7 24.8 %collective-permute-start.20 = (f32[2,20,1,64]{3,2,1,0:T(1,128)S(1)}, f32[2,20,1,64]{3,2,1,0:T(1,128)S(1)}, u32[]{:S(2)}, u32[]{:S(2)}) collective-permute-start(f32[2,20,1,64]{3,2,1,0:T(1,128)S(1)} %broadcast.9299), channel_id=1, source_target_pairs={{16,0},{32,16},{48,32},{64,48},{80,64},{96,80},{112,96},{128,112},... | collective-permute-start | bytes 30728 | tf_op jit(solution)/shard_map/ppermute | solution.py:27
  7.1 18.3 %collective-permute-start.21 = (f32[2,20,1,64]{3,2,1,0:T(1,128)S(1)}, f32[2,20,1,64]{3,2,1,0:T(1,128)S(1)}, u32[]{:S(2)}, u32[]{:S(2)}) collective-permute-start(f32[2,20,1,64]{3,2,1,0:T(1,128)S(1)} %broadcast.9299), channel_id=1, source_target_pairs={{0,16},{16,32},{32,48},{48,64},{64,80},{80,96},{96,112},{112,128},... | collective-permute-start | bytes 30728 | tf_op jit(solution)/shard_map/ppermute | solution.py:25
  10.1 23.4 %collective-permute-start.1 = (f32[2,20,1,128]{3,2,1,0:T(1,128)S(1)}, f32[2,20,1,128]{3,2,1,0:T(1,128)S(1)}, u32[]{:S(2)}, u32[]{:S(2)}) collective-permute-start(f32[2,20,1,128]{3,2,1,0:T(1,128)S(1)} %get-tuple-element.368), channel_id=1, source_target_pairs={{0,16},{16,32},{32,48},{48,64},{64,80},{80,96},{96,112},{112,128},... | collective-permute-start | bytes 61448 | tf_op jit(solution)/shard_map/ppermute | solution.py:25
  14.2 19.3 %collective-permute-start = (f32[2,20,1,128]{3,2,1,0:T(1,128)S(1)}, f32[2,20,1,128]{3,2,1,0:T(1,128)S(1)}, u32[]{:S(2)}, u32[]{:S(2)}) collective-permute-start(f32[2,20,1,128]{3,2,1,0:T(1,128)S(1)} %get-tuple-element.367), channel_id=1, source_target_pairs={{16,0},{32,16},{48,32},{64,48},{80,64},{96,80},{112,96},{128,112},... | collective-permute-start | bytes 61448 | tf_op jit(solution)/shard_map/ppermute | solution.py:27
  25.8 12.3 %collective-permute-start.22 = (f32[2,20,6,1]{3,0,2,1:T(2,128)S(1)}, f32[2,20,6,1]{3,0,2,1:T(2,128)S(1)}, u32[]{:S(2)}, u32[]{:S(2)}) collective-permute-start(f32[2,20,6,1]{3,0,2,1:T(2,128)S(1)} %get-tuple-element.385), channel_id=1, source_target_pairs={{1,0},{2,1},{3,2},{4,3},{5,4},{6,5},{7,6},{8,7},{9,8},{10,9},{11,1... | collective-permute-start | bytes 2888 | tf_op jit(solution)/shard_map/ppermute | solution.py:27
  35.7 10.6 %collective-permute-start.2 = (f32[2,20,10,1]{3,2,1,0:T(8,128)S(1)}, f32[2,20,10,1]{3,2,1,0:T(8,128)S(1)}, u32[]{:S(2)}, u32[]{:S(2)}) collective-permute-start(f32[2,20,10,1]{3,2,1,0:T(8,128)S(1)} %get-tuple-element.320), channel_id=1, source_target_pairs={{1,0},{2,1},{3,2},{4,3},{5,4},{6,5},{7,6},{8,7},{9,8},{10,9},{11,1... | collective-permute-start | bytes 4808 | tf_op jit(solution)/shard_map/ppermute | solution.py:27
  47.4 30.7 %collective-permute-start.4 = (f32[20,1,128]{2,1,0:T(1,128)}, f32[20,1,128]{2,1,0:T(1,128)S(1)}, u32[]{:S(2)}, u32[]{:S(2)}) collective-permute-start(f32[20,1,128]{2,1,0:T(1,128)} %get-tuple-element.400), channel_id=1, source_target_pairs={{16,0},{32,16},{48,32},{64,48},{80,64},{96,80},{112,96},{128,112},... | collective-permute-start | bytes 30728 | tf_op jit(solution)/shard_map/ppermute | solution.py:27
  52.1 25.9 %collective-permute-start.5 = (f32[20,1,128]{2,1,0:T(1,128)S(1)}, f32[20,1,128]{2,1,0:T(1,128)S(1)}, u32[]{:S(2)}, u32[]{:S(2)}) collective-permute-start(f32[20,1,128]{2,1,0:T(1,128)S(1)} %get-tuple-element.399), channel_id=1, source_target_pairs={{0,16},{16,32},{32,48},{48,64},{64,80},{80,96},{96,112},{112,128},... | collective-permute-start | bytes 30728 | tf_op jit(solution)/shard_map/ppermute | solution.py:25
  60.5 9.6 %collective-permute-start.17 = (f32[20,1,64]{2,1,0:T(1,128)S(1)}, f32[20,1,64]{2,1,0:T(1,128)S(1)}, u32[]{:S(2)}, u32[]{:S(2)}) collective-permute-start(f32[20,1,64]{2,1,0:T(1,128)S(1)} %get-tuple-element.425), channel_id=1, source_target_pairs={{0,16},{16,32},{32,48},{48,64},{64,80},{80,96},{96,112},{112,128},... | collective-permute-start | bytes 15368 | tf_op jit(solution)/shard_map/ppermute | solution.py:25
  70.3 12.2 %collective-permute-start.18 = (f32[20,6,1]{2,0,1:T(8,128)S(1)}, f32[20,6,1]{2,0,1:T(8,128)S(1)}, u32[]{:S(2)}, u32[]{:S(2)}) collective-permute-start(f32[20,6,1]{2,0,1:T(8,128)S(1)} %get-tuple-element.422), channel_id=1, source_target_pairs={{1,0},{2,1},{3,2},{4,3},{5,4},{6,5},{7,6},{8,7},{9,8},{10,9},{11,1... | collective-permute-start | bytes 1448 | tf_op jit(solution)/shard_map/ppermute | solution.py:27
  72.3 10.3 %collective-permute-start.19 = (f32[20,6,1]{2,0,1:T(8,128)S(1)}, f32[20,6,1]{2,0,1:T(8,128)S(1)}, u32[]{:S(2)}, u32[]{:S(2)}) collective-permute-start(f32[20,6,1]{2,0,1:T(8,128)S(1)} %get-tuple-element.423), channel_id=1, source_target_pairs={{0,1},{1,2},{2,3},{3,4},{4,5},{5,6},{6,7},{7,8},{8,9},{9,10},{10,1... | collective-permute-start | bytes 1448 | tf_op jit(solution)/shard_map/ppermute | solution.py:25
  91.6 9.6 %collective-permute-start.8 = (f32[2,20,1,128]{3,2,1,0:T(1,128)S(1)}, f32[2,20,1,128]{3,2,1,0:T(1,128)S(1)}, u32[]{:S(2)}, u32[]{:S(2)}) collective-permute-start(f32[2,20,1,128]{3,2,1,0:T(1,128)S(1)} %get-tuple-element.360), channel_id=1, source_target_pairs={{16,0},{32,16},{48,32},{64,48},{80,64},{96,80},{112,96},{128,112},... | collective-permute-start | bytes 61448 | tf_op jit(solution)/shard_map/ppermute | solution.py:27
  109.8 10.5 %collective-permute-start.10 = (f32[2,20,10,1]{3,2,1,0:T(8,128)S(1)}, f32[2,20,10,1]{3,2,1,0:T(8,128)S(1)}, u32[]{:S(2)}, u32[]{:S(2)}) collective-permute-start(f32[2,20,10,1]{3,2,1,0:T(8,128)S(1)} %get-tuple-element.318), channel_id=1, source_target_pairs={{1,0},{2,1},{3,2},{4,3},{5,4},{6,5},{7,6},{8,7},{9,8},{10,9},{11,1... | collective-permute-start | bytes 4808 | tf_op jit(solution)/shard_map/ppermute | solution.py:27
  134.5 10.6 %collective-permute-start.14 = (f32[2,20,10,1]{3,2,1,0:T(8,128)S(1)}, f32[2,20,10,1]{3,2,1,0:T(8,128)S(1)}, u32[]{:S(2)}, u32[]{:S(2)}) collective-permute-start(f32[2,20,10,1]{3,2,1,0:T(8,128)S(1)} %get-tuple-element.316), channel_id=1, source_target_pairs={{1,0},{2,1},{3,2},{4,3},{5,4},{6,5},{7,6},{8,7},{9,8},{10,9},{11,1... | collective-permute-start | bytes 4808 | tf_op jit(solution)/shard_map/ppermute | solution.py:27
  170.2 9.2 %collective-permute-start.29 = (f32[2,20,1,64]{3,2,1,0:T(1,128)S(1)}, f32[2,20,1,64]{3,2,1,0:T(1,128)S(1)}, u32[]{:S(2)}, u32[]{:S(2)}) collective-permute-start(f32[2,20,1,64]{3,2,1,0:T(1,128)S(1)} %get-tuple-element.392), channel_id=1, source_target_pairs={{0,16},{16,32},{32,48},{48,64},{64,80},{80,96},{96,112},{112,128},... | collective-permute-start | bytes 30728 | tf_op jit(solution)/shard_map/ppermute | solution.py:25
  180.5 9.9 %collective-permute-start.30 = (f32[2,20,6,1]{3,0,2,1:T(2,128)S(1)}, f32[2,20,6,1]{3,0,2,1:T(2,128)S(1)}, u32[]{:S(2)}, u32[]{:S(2)}) collective-permute-start(f32[2,20,6,1]{3,0,2,1:T(2,128)S(1)} %get-tuple-element.377), channel_id=1, source_target_pairs={{1,0},{2,1},{3,2},{4,3},{5,4},{6,5},{7,6},{8,7},{9,8},{10,9},{11,1... | collective-permute-start | bytes 2888 | tf_op jit(solution)/shard_map/ppermute | solution.py:27
  182.4 9.2 %collective-permute-start.31 = (f32[2,20,6,1]{3,0,2,1:T(2,128)S(1)}, f32[2,20,6,1]{3,0,2,1:T(2,128)S(1)}, u32[]{:S(2)}, u32[]{:S(2)}) collective-permute-start(f32[2,20,6,1]{3,0,2,1:T(2,128)S(1)} %get-tuple-element.378), channel_id=1, source_target_pairs={{0,1},{1,2},{2,3},{3,4},{4,5},{5,6},{6,7},{7,8},{8,9},{9,10},{10,1... | collective-permute-start | bytes 2888 | tf_op jit(solution)/shard_map/ppermute | solution.py:25
  193.0 10.1 %collective-permute-start.33 = (f32[2,20,1,64]{3,2,1,0:T(1,128)S(1)}, f32[2,20,1,64]{3,2,1,0:T(1,128)S(1)}, u32[]{:S(2)}, u32[]{:S(2)}) collective-permute-start(f32[2,20,1,64]{3,2,1,0:T(1,128)S(1)} %get-tuple-element.388), channel_id=1, source_target_pairs={{0,16},{16,32},{32,48},{48,64},{64,80},{80,96},{96,112},{112,128},... | collective-permute-start | bytes 30728 | tf_op jit(solution)/shard_map/ppermute | solution.py:25
  204.2 9.5 %collective-permute-start.34 = (f32[2,20,6,1]{3,0,2,1:T(2,128)S(1)}, f32[2,20,6,1]{3,0,2,1:T(2,128)S(1)}, u32[]{:S(2)}, u32[]{:S(2)}) collective-permute-start(f32[2,20,6,1]{3,0,2,1:T(2,128)S(1)} %get-tuple-element.373), channel_id=1, source_target_pairs={{1,0},{2,1},{3,2},{4,3},{5,4},{6,5},{7,6},{8,7},{9,8},{10,9},{11,1... | collective-permute-start | bytes 2888 | tf_op jit(solution)/shard_map/ppermute | solution.py:27
  216.9 10.1 %collective-permute-start.36 = (f32[2,20,1,128]{3,2,1,0:T(1,128)S(1)}, f32[2,20,1,128]{3,2,1,0:T(1,128)S(1)}, u32[]{:S(2)}, u32[]{:S(2)}) collective-permute-start(f32[2,20,1,128]{3,2,1,0:T(1,128)S(1)} %get-tuple-element.352), channel_id=1, source_target_pairs={{16,0},{32,16},{48,32},{64,48},{80,64},{96,80},{112,96},{128,112},... | collective-permute-start | bytes 61448 | tf_op jit(solution)/shard_map/ppermute | solution.py:27
  233.4 11.3 %collective-permute-start.39 = (f32[2,20,10,1]{3,2,1,0:T(8,128)S(1)}, f32[2,20,10,1]{3,2,1,0:T(8,128)S(1)}, u32[]{:S(2)}, u32[]{:S(2)}) collective-permute-start(f32[2,20,10,1]{3,2,1,0:T(8,128)S(1)} %get-tuple-element.315), channel_id=1, source_target_pairs={{0,1},{1,2},{2,3},{3,4},{4,5},{5,6},{6,7},{7,8},{8,9},{9,10},{10,1... | collective-permute-start | bytes 4808 | tf_op jit(solution)/shard_map/ppermute | solution.py:25
  240.7 10.5 %collective-permute-start.38 = (f32[2,20,10,1]{3,2,1,0:T(8,128)S(1)}, f32[2,20,10,1]{3,2,1,0:T(8,128)S(1)}, u32[]{:S(2)}, u32[]{:S(2)}) collective-permute-start(f32[2,20,10,1]{3,2,1,0:T(8,128)S(1)} %get-tuple-element.314), channel_id=1, source_target_pairs={{1,0},{2,1},{3,2},{4,3},{5,4},{6,5},{7,6},{8,7},{9,8},{10,9},{11,1... | collective-permute-start | bytes 4808 | tf_op jit(solution)/shard_map/ppermute | solution.py:27
  265.4 10.5 %collective-permute-start.42 = (f32[2,20,10,1]{3,2,1,0:T(8,128)S(1)}, f32[2,20,10,1]{3,2,1,0:T(8,128)S(1)}, u32[]{:S(2)}, u32[]{:S(2)}) collective-permute-start(f32[2,20,10,1]{3,2,1,0:T(8,128)S(1)} %get-tuple-element.312), channel_id=1, source_target_pairs={{1,0},{2,1},{3,2},{4,3},{5,4},{6,5},{7,6},{8,7},{9,8},{10,9},{11,1... | collective-permute-start | bytes 4808 | tf_op jit(solution)/shard_map/ppermute | solution.py:27
  290.8 10.5 %collective-permute-start.46 = (f32[2,20,10,1]{3,2,1,0:T(8,128)S(1)}, f32[2,20,10,1]{3,2,1,0:T(8,128)S(1)}, u32[]{:S(2)}, u32[]{:S(2)}) collective-permute-start(f32[2,20,10,1]{3,2,1,0:T(8,128)S(1)} %get-tuple-element.310), channel_id=1, source_target_pairs={{1,0},{2,1},{3,2},{4,3},{5,4},{6,5},{7,6},{8,7},{9,8},{10,9},{11,1... | collective-permute-start | bytes 4808 | tf_op jit(solution)/shard_map/ppermute | solution.py:27
  (56 other events, 407.2 us)
where the time goes:
time: 304 us; the launch traced here: 302 us
  starting transfers between devices  177 us (58%)
  waiting for transfers between devices  87.4 us (29%)
  other arithmetic  17.9 us (6%)
  local copies, waits for them, and re-layouts  16.8 us (6%)
    ppermute x24, starting transfers between devices, extended(): lax.ppermute(head, axis, [((i + 1) % count, i) for i in range(ends)])  89.4 us
    ppermute x24, starting transfers between devices, extended(): lax.ppermute(tail, axis, [(i, (i + 1) % count) for i in range(ends)])  88 us
    ppermute x24, waiting for transfers between devices, extended(): lax.ppermute(head, axis, [((i + 1) % count, i) for i in range(ends)])  50.1 us
    ppermute x24, waiting for transfers between devices, extended(): lax.ppermute(tail, axis, [(i, (i + 1) % count) for i in range(ends)])  37.3 us
    unnamed x144, local copies, waits for them, and re-layouts  6.85 us
  transfers between devices with their start and end apart: 48, of which 28 were waited for; matrix products, arithmetic and copies ran while one was open for 5% of the time, Pallas kernels for 0%

commit v1 on v0

v1 whole, which is shorter than its diff:
```python
import jax
import jax.numpy as jnp
from jax import lax
from jax.experimental import pallas as pl
from jax.experimental.pallas import tpu as pltpu
from jax.sharding import PartitionSpec as P

L = 20
PLANES = 45
STRIPS = 12
F32 = jnp.float32


def iotas(shape=(8, 128)):
    return lax.broadcasted_iota(jnp.int32, shape, 0), lax.broadcasted_iota(jnp.int32, shape, 1)


def pack_kernel(vel, drive, stiff, thick, ice, cls, table, main, strips):
    sub, lane = iotas()
    m = ice[...].astype(F32)
    drag = jnp.zeros((8, 128), F32)
    for i in range(8):
        drag = jnp.where(cls[...] == i, table[i], drag)

    def plane(p):
        if p < 40:
            return vel[p // L, p % L] * m
        return (drive[0] * m, drive[1] * m, 0.5 * stiff[...] * m, thick[...], drag * m)[p - 40]

    for j in range(STRIPS):
        packed = jnp.zeros((8, 128), F32)
        for g in range(4):
            p = 4 * j + g
            if p < PLANES:
                tile = pltpu.roll(plane(p), 4, 0)
                main[p] = tile
                moved = pltpu.roll(tile, (32 * g + 16) % 128, 1)
                packed = jnp.where((lane >= 32 * g) & (lane < 32 * g + 32), moved, packed)
        strips[j] = packed


def neighbours(tiles, sub, lane):
    n = len(tiles[0])
    rows, cols = [], []
    for lt in range(len(tiles)):
        r, c = [], []
        for k in range(n):
            here = tiles[lt][k]
            up = pltpu.roll(jnp.where(sub == 7, tiles[lt][(k - 1) % n], here), 1, 0)
            dn = pltpu.roll(jnp.where(sub == 0, tiles[lt][(k + 1) % n], here), 7, 0)
            r.append((up, dn))
            if len(tiles) == 2:
                other = tiles[1 - lt][k]
                lf = pltpu.roll(jnp.where(lane == 127, other, here), 1, 1)
                rt = pltpu.roll(jnp.where(lane == 0, other, here), 127, 1)
            else:
                lf = pltpu.roll(here, 1, 1)
                rt = pltpu.roll(here, 127, 1)
            c.append((lf, rt))
        rows.append(r)
        cols.append(c)
    return rows, cols


def weighted(component, row_pair, col_pair):
    a = row_pair[0] + row_pair[1]
    b = col_pair[0] + col_pair[1]
    return 4.0 * a + b if component == 0 else a + 4.0 * b


def main_kernel(
    gm2, gm1, g0, gp1, gp2, restrict, expand, vel_out, res_out,
    V, F, Q, E, W, D, C, I, T, X, CA, CB, CE, CF, CX, CQ, CW, CC, CI, CT, PC,
):
    sub, lane = iotas()
    low = sub < 4
    G = [gm2, gm1, g0, gp1, gp2]
    inner = (lane < 16) | (lane >= 112)

    for p in range(PLANES):
        for k in range(5):
            a, b = G[k], G[(k + 1) % 5]
            main = jnp.where(low, a[p], b[p])
            j, g = PLANES + p // 4, p % 4
            rim = jnp.where(low, a[j], b[j])
            rim = pltpu.roll(rim, 128 - (32 * g + 16), 1)
            rim = jnp.where(inner, rim, 0.0)
            for lt, tile in ((0, main), (1, rim)):
                if p < 40:
                    V[p, lt, 8 * k : 8 * k + 8, :] = tile
                else:
                    if p == 43:
                        tile = jnp.where(tile > 0.0, tile, 1.0)
                    F[p - 40, lt, 8 * k : 8 * k + 8, :] = tile

    def rows(k):
        return slice(8 * k, 8 * k + 8)

    root = [[jnp.sqrt(F[2, lt, rows(k), :]) for k in range(5)] for lt in range(2)]
    quarter = [[25.0 / (F[3, lt, rows(k), :] * F[3, lt, rows(k), :]) for k in range(5)] for lt in range(2)]
    for lt in range(2):
        for k in range(5):
            T[0, lt, rows(k), :] = root[lt][k]
            T[1, lt, rows(k), :] = quarter[lt][k]

    def visc(z, _):
        after, before = jnp.minimum(z + 1, L - 1), jnp.maximum(z - 1, 0)
        u = [[V[z, lt, rows(k), :] for k in range(5)] for lt in range(2)]
        ur, uc = neighbours(u, sub, lane)
        ux = [[ur[lt][k][1] - ur[lt][k][0] for k in range(5)] for lt in range(2)]
        uy = [[uc[lt][k][1] - uc[lt][k][0] for k in range(5)] for lt in range(2)]
        v = [[V[z + L, lt, rows(k), :] for k in range(5)] for lt in range(2)]
        vr, vc = neighbours(v, sub, lane)
        for lt in range(2):
            for k in range(5):
                vx = vr[lt][k][1] - vr[lt][k][0]
                vy = vc[lt][k][1] - vc[lt][k][0]
                uz = V[after, lt, rows(k), :] - V[before, lt, rows(k), :]
                vz = V[after + L, lt, rows(k), :] - V[before + L, lt, rows(k), :]
                x, y = ux[lt][k], uy[lt][k]
                shear = y + vx
                plane = x * x + vy * vy + x * vy + 0.25 * (shear * shear)
                eps = 0.25 * plane + T[1, lt, rows(k), :] * (uz * uz + vz * vz) + 0.01
                q = T[0, lt, rows(k), :] * jnp.exp(jnp.log(eps) * (-1.0 / 6.0))
                Q[z, lt, rows(k), :] = q
                if k < 4:
                    E[z, lt, rows(k), :] = q * q
        return 0

    lax.fori_loop(0, L, visc, 0)

    def factor(z, carry):
        top = jnp.where(z < L - 1, 1.0, 0.0)
        bed = jnp.where(z == 0, 1.0, 0.0)
        after = jnp.minimum(z + 1, L - 1)
        q = [[Q[z, lt, rows(k), :] for k in range(5)] for lt in range(2)]
        qr, qc = neighbours(q, sub, lane)
        out = []
        for lt in range(2):
            for k in range(4):
                i = lt * 4 + k
                wbefore, cx, cy = carry[3 * i : 3 * i + 3]
                h = F[3, lt, rows(k), :]
                ih = 20.0 / h
                w = (E[z, lt, rows(k), :] + E[after, lt, rows(k), :]) * (0.5 * top * (ih * ih))
                off = jnp.where(F[2, lt, rows(k), :] > 0.0, 0.0, 1.0)
                common = w + wbefore + bed * (F[4, lt, rows(k), :] * ih) + off
                W[z, lt, rows(k), :] = w
                new = [w]
                for component, cb in ((0, cx), (1, cy)):
                    d = q[lt][k] * weighted(component, qr[lt][k], qc[lt][k]) + common
                    inv = 1.0 / (d - wbefore * cb)
                    c = w * inv
                    D[component * L + z, lt, rows(k), :] = d
                    I[component * L + z, lt, rows(k), :] = inv
                    C[component * L + z, lt, rows(k), :] = c
                    new.append(c)
                out += new
        return tuple(out)

    zero = jnp.zeros((8, 128), F32)
    lax.fori_loop(0, L, factor, (zero,) * 24)

    def forward(src, tiles, rim_tile):
        n = len(tiles)
        use = tiles + ([rim_tile] if rim_tile is not None else [])

        def step(z, carry):
            out = []
            for component in range(2):
                p = component * L + z
                q = [[Q[z, lt, rows(k), :] for k in use] for lt in range(2)]
                y = [[q[lt][i] * src[p, lt, rows(k), :] for i, k in enumerate(use)] for lt in range(2)]
                yr, yc = neighbours(y, sub, lane)
                for lt in range(2):
                    for i, k in enumerate(tiles):
                        t = F[component, lt, rows(k), :] + q[lt][i] * weighted(component, yr[lt][i], yc[lt][i])
                        t = t + carry[(component * 2 + lt) * n + i]
                        T[p, lt, rows(k), :] = t
                        out.append(C[p, lt, rows(k), :] * t)
            return tuple(out)

        lax.fori_loop(0, L, step, (zero,) * (4 * n))

    def backward(src, dst, tiles):
        n = len(tiles)

        def step(s, carry):
            z = L - 1 - s
            out = []
            for component in range(2):
                p = component * L + z
                for lt in range(2):
                    for i, k in enumerate(tiles):
                        new = I[p, lt, rows(k), :] * T[p, lt, rows(k), :] + C[p, lt, rows(k), :] * carry[(component * 2 + lt) * n + i]
                        dst[p, lt, rows(k), :] = 0.2 * src[p, lt, rows(k), :] + 0.8 * new
                        out.append(new)
            return tuple(out)

        lax.fori_loop(0, L, step, (zero,) * (4 * n))

    def remainder(src, tiles, put):
        n = len(tiles)

        def step(z, carry):
            after = jnp.minimum(z + 1, L - 1)
            out = []
            for component in range(2):
                p = component * L + z
                x = [[src[p, lt, rows(k), :] for k in tiles] for lt in range(2)]
                q = [[Q[z, lt, rows(k), :] for k in tiles] for lt in range(2)]
                y = [[q[lt][i] * x[lt][i] for i in range(n)] for lt in range(2)]
                yr, yc = neighbours(y, sub, lane)
                got = []
                for lt in range(2):
                    for i, k in enumerate(tiles):
                        w = W[z, lt, rows(k), :]
                        r = F[component, lt, rows(k), :] + q[lt][i] * weighted(component, yr[lt][i], yc[lt][i])
                        r = r - D[p, lt, rows(k), :] * x[lt][i]
                        r = r + w * src[after + component * L, lt, rows(k), :] + carry[(component * 2 + lt) * n + i]
                        got.append(r)
                        out.append(w * x[lt][i])
                put(component, z, got)
            return tuple(out)

        lax.fori_loop(0, L, step, (zero,) * (4 * n))

    pre = [0, 1, 2, 3]
    forward(V, pre, 4)
    backward(V, X, pre)
    forward(X, pre, None)
    backward(X, X, pre)

    def put_rem(component, z, got):
        for lt in range(2):
            for i, k in enumerate(pre):
                T[component * L + z, lt, rows(k), :] = got[lt * 4 + i]

    remainder(X, pre, put_rem)

    even, odd = pl.ds(0, 16, stride=2), pl.ds(1, 16, stride=2)

    def gather(p, _):
        for lt in range(2):
            CA[lt, pl.ds(pl.multiple_of(p * 16, 16), 16), :] = T[p, lt, even, :] + T[p, lt, odd, :]
        return 0

    lax.fori_loop(0, 40, gather, 0)

    def gather_eta(z, _):
        for lt in range(2):
            CA[lt, pl.ds(pl.multiple_of((z + 40) * 16, 16), 16), :] = E[z, lt, even, :] + E[z, lt, odd, :]
        return 0

    lax.fori_loop(0, L, gather_eta, 0)
    for i in range(3):
        for lt in range(2):
            CA[lt, (60 + i) * 16 : (61 + i) * 16, :] = F[2 + i, lt, even, :] + F[2 + i, lt, odd, :]
    CB[...] = jnp.dot(
        CA[0], restrict[0], precision=lax.Precision.HIGHEST, preferred_element_type=F32
    ) + jnp.dot(CA[1], restrict[1], precision=lax.Precision.HIGHEST, preferred_element_type=F32)

    cmask = [jnp.where(CB[960 + 8 * k : 968 + 8 * k, :] > 0.0, 0.0, 1.0) for k in range(2)]
    cthick = [CB[976 + 8 * k : 984 + 8 * k, :] for k in range(2)]
    cih = [20.0 / jnp.where(t > 0.0, t, 1.0) for t in cthick]
    cdrag = [CB[992 + 8 * k : 1000 + 8 * k, :] * cih[k] for k in range(2)]

    def at(p, k):
        return pl.ds(pl.multiple_of(p * 16 + 8 * k, 8), 8)

    def coarse_factor(z, carry):
        top = jnp.where(z < L - 1, 1.0, 0.0)
        bed = jnp.where(z == 0, 1.0, 0.0)
        after = jnp.minimum(z + 1, L - 1)
        e = [CB[at(40 + z, k), :] for k in range(2)]
        q = [[0.5 * jnp.sqrt(e[k]) for k in range(2)]]
        qr, qc = neighbours(q, sub, lane)
        out = []
        for k in range(2):
            wbefore, cx, cy = carry[3 * k : 3 * k + 3]
            w = (e[k] + CB[at(40 + after, k), :]) * (0.5 * top * (cih[k] * cih[k]))
            common = w + wbefore + bed * cdrag[k] + cmask[k]
            CQ[at(z, k), :] = q[0][k]
            new = [w]
            for component, cb in ((0, cx), (1, cy)):
                d = q[0][k] * weighted(component, qr[0][k], qc[0][k]) + common
                inv = 1.0 / (d - wbefore * cb)
                c = w * inv
                CI[at(component * L + z, k), :] = inv
                CC[at(component * L + z, k), :] = c
                new.append(c)
            out += new
        return tuple(out)

    lax.fori_loop(0, L, coarse_factor, (zero,) * 6)

    for turn in range(4):

        def coarse_forward(z, carry, turn=turn):
            out = []
            for component in range(2):
                p = component * L + z
                if turn > 0:
                    q = [CQ[at(z, k), :] for k in range(2)]
                    y = [[q[k] * CX[at(p, k), :] for k in range(2)]]
                    yr, yc = neighbours(y, sub, lane)
                for k in range(2):
                    t = CB[at(p, k), :] + carry[component * 2 + k]
                    if turn > 0:
                        t = t + q[k] * weighted(component, yr[0][k], yc[0][k])
                    CT[at(p, k), :] = t
                    out.append(CC[at(p, k), :] * t)
            return tuple(out)

        lax.fori_loop(0, L, coarse_forward, (zero,) * 4)

        def coarse_backward(s, carry, turn=turn):
            z = L - 1 - s
            out = []
            for component in range(2):
                p = component * L + z
                for k in range(2):
                    new = CI[at(p, k), :] * CT[at(p, k), :] + CC[at(p, k), :] * carry[component * 2 + k]
                    if turn > 0:
                        CX[at(p, k), :] = 0.2 * CX[at(p, k), :] + 0.8 * new
                    else:
                        CX[at(p, k), :] = 0.8 * new
                    out.append(new)
            return tuple(out)

        lax.fori_loop(0, L, coarse_backward, (zero,) * 4)

    def spread(p, _):
        CE[pl.ds(pl.multiple_of(p * 8, 8), 8), :] = pltpu.roll(
            jnp.where(low, CX[at(p, 1), :], CX[at(p, 0), :]), 4, 0
        )
        return 0

    lax.fori_loop(0, 40, spread, 0)
    for lt in range(2):
        CF[lt] = jnp.dot(CE[...], expand[lt], precision=lax.Precision.HIGHEST, preferred_element_type=F32)

    def correct(p, _):
        for lt in range(2):
            tile = CF[lt, pl.ds(pl.multiple_of(p * 8, 8), 8), :]
            PC[p, lt, pl.ds(0, 8, stride=2), :] = tile
            PC[p, lt, pl.ds(1, 8, stride=2), :] = tile
            for k in (1, 2):
                m = jnp.where(F[2, lt, rows(k), :] > 0.0, 1.0, 0.0)
                X[p, lt, rows(k), :] = X[p, lt, rows(k), :] + m * PC[p, lt, rows(k - 1), :]
        return 0

    lax.fori_loop(0, 40, correct, 0)

    post = [1, 2]
    for _ in range(2):
        forward(X, post, None)
        backward(X, X, post)

    def put_res(component, z, got):
        res_out[component, z] = pltpu.roll(jnp.where(low, got[1], got[0]), 4, 0)
        p = component * L + z
        vel_out[component, z] = pltpu.roll(jnp.where(low, X[p, 0, rows(2), :], X[p, 0, rows(1), :]), 4, 0)

    remainder(X, post, put_res)


def transfer_matrices():
    lane = jnp.arange(128)
    main = lane // 2
    rim = jnp.where(lane < 16, 64 + lane // 2, jnp.where(lane >= 112, 120 + (lane - 112) // 2, -1))
    hits = jnp.stack([main, rim])[:, :, None] == lane[None, None, :]
    restrict = jnp.where(hits, 0.25, 0.0).astype(F32)
    expand = jnp.where(hits, 1.0, 0.0).astype(F32).transpose(0, 2, 1)
    return restrict, expand


def shift(axis, by):
    count = lax.axis_size(axis)
    return [(i, i + by) for i in range(count) if 0 <= i + by < count]


def per_device(velocity, drive, stiffness, thickness, ice_mask, friction_class, friction_table):
    vmem = pl.BlockSpec(memory_space=pltpu.VMEM)
    smem = pl.BlockSpec(memory_space=pltpu.SMEM)
    main, strips = pl.pallas_call(
        pack_kernel,
        out_shape=(jax.ShapeDtypeStruct((PLANES, 8, 128), F32), jax.ShapeDtypeStruct((STRIPS, 8, 128), F32)),
        in_specs=[vmem] * 6 + [smem],
        out_specs=(vmem, vmem),
        name="pack",
    )(velocity, drive, stiffness, thickness, ice_mask, friction_class, friction_table)
    left = lax.ppermute(strips, "gy", shift("gy", 1))
    right = lax.ppermute(strips, "gy", shift("gy", -1))
    lane = lax.broadcasted_iota(jnp.int32, strips.shape, 2)
    rim = jnp.where(lane % 32 < 16, left, right)
    whole = jnp.concatenate([main, rim], axis=0)
    parts = [whole if by == 0 else lax.ppermute(whole, "gx", shift("gx", -by)) for by in (-2, -1, 0, 1, 2)]
    restrict, expand = transfer_matrices()
    fine = lambda n, r: pltpu.VMEM((n, 2, r, 128), F32)
    coarse = lambda n: pltpu.VMEM((16 * n, 128), F32)
    out = jax.ShapeDtypeStruct((2, L, 8, 128), F32)
    return pl.pallas_call(
        main_kernel,
        out_shape=(out, out),
        in_specs=[vmem] * 7,
        out_specs=(vmem, vmem),
        scratch_shapes=[
            fine(40, 40), fine(5, 40), fine(20, 40), fine(20, 32), fine(20, 32), fine(40, 32), fine(40, 32), fine(40, 32),
            fine(40, 40), fine(40, 32),
            pltpu.VMEM((2, 63 * 16, 128), F32), coarse(63), pltpu.VMEM((320, 128), F32), pltpu.VMEM((2, 320, 128), F32),
            coarse(40), coarse(20), coarse(20), coarse(40), coarse(40), coarse(40), fine(40, 16),
        ],
        compiler_params=pltpu.CompilerParams(vmem_limit_bytes=48 * 1024 * 1024),
        name="cycle",
    )(*parts, restrict, expand)


def solution(mesh):
    return jax.shard_map(
        per_device,
        mesh=mesh,
        in_specs=(
            P(None, None, "gx", "gy"),
            P(None, "gx", "gy"),
            P("gx", "gy"),
            P("gx", "gy"),
            P("gx", "gy"),
            P("gx", "gy"),
            P(),
        ),
        out_specs=(P(None, None, "gx", "gy"), P(None, None, "gx", "gy")),
        check_vma=False,
    )
```

time: 304 us -> 67.4 us (0.22)
  the two profiles are of different devices: /device:TPU:391 before, /device:TPU:406 now
where the time goes in v1:
time: 67.4 us; the launch traced here: 67.1 us
  Pallas kernels  31.9 us (47%)
  starting transfers between devices  18.6 us (28%)
  waiting for transfers between devices  14.8 us (22%)
  other arithmetic  1.08 us (2%)
  between operations  0.74 us (1%)
    pallas_call x1, Pallas kernels, per_device(): pl.pallas_call(main_kernel, out_shape=(out, out), in_specs=[vmem] * 7, ou...  30.2 us
    ppermute x4, starting transfers between devices, per_device(): lax.ppermute(whole, 'gx', shift('gx', -by))  14.3 us
    ppermute x4, waiting for transfers between devices, per_device(): lax.ppermute(whole, 'gx', shift('gx', -by))  11.3 us
    ppermute x1, waiting for transfers between devices, per_device(): left = lax.ppermute(strips, 'gy', shift('gy', 1))  3.41 us
    ppermute x1, starting transfers between devices, per_device(): right = lax.ppermute(strips, 'gy', shift('gy', -1))  2.16 us
    ppermute x1, starting transfers between devices, per_device(): left = lax.ppermute(strips, 'gy', shift('gy', 1))  2.15 us
    pallas_call x1, Pallas kernels, per_device(): pl.pallas_call(pack_kernel, out_shape=(jax.ShapeDtypeStruct((PLANES, 8, 1...  1.71 us
  transfers between devices with their start and end apart: 6, of which 4 were waited for; matrix products, arithmetic and copies ran while one was open for 0% of the time, Pallas kernels for 0%

profile of v1, /device:TPU:406, one launch (start us, length us, event | category | flops | bytes accessed | tf_op | source)
XLA Modules:
  0.0 67.1 jit_solution(3171823414979295922)
XLA Ops:
  0.6 1.7 %pack.1 = (f32[45,8,128]{2,1,0:T(8,128)}, f32[12,8,128]{2,1,0:T(8,128)}) custom-call(f32[2,20,8,128]{3,2,1,0:T(8,128)} %vel.1, f32[2,8,128]{2,1,0:T(8,128)} %drive.1, f32[8,128]{1,0:T(8,128)} %stiff.1, f32[8,128]{1,0:T(8,128)} %thick.1, s32[8,128]{1,0:T(8,128)} %ice.1, s32[8,128]{1,0:T(8,128)} %cls.1, f32[8]{0:T(128)} %table.1), custom_call_target="tpu_custom_call" | custom-call | tf_op jit(solution)/shard_map/pack/pallas_call | solution.py:386
  2.3 2.2 %collective-permute-start.1 = (f32[12,8,128]{2,1,0:T(8,128)}, f32[12,8,128]{2,1,0:T(8,128)S(1)}, u32[]{:S(2)}, u32[]{:S(2)}) collective-permute-start(f32[12,8,128]{2,1,0:T(8,128)} %get-tuple-element.5), channel_id=1, source_target_pairs={{1,0},{2,1},{3,2},{4,3},{5,4},{6,5},{7,6},{8,7},{9,8},{10,9},{11,1... | collective-permute-start | bytes 147464 | tf_op jit(solution)/shard_map/ppermute | solution.py:394
  4.5 2.1 %collective-permute-start = (f32[12,8,128]{2,1,0:T(8,128)}, f32[12,8,128]{2,1,0:T(8,128)S(1)}, u32[]{:S(2)}, u32[]{:S(2)}) collective-permute-start(f32[12,8,128]{2,1,0:T(8,128)} %get-tuple-element.5), channel_id=1, source_target_pairs={{0,1},{1,2},{2,3},{3,4},{4,5},{5,6},{6,7},{7,8},{8,9},{9,10},{10,1... | collective-permute-start | bytes 147464 | tf_op jit(solution)/shard_map/ppermute | solution.py:393
  6.7 0.0 collective-permute-done.1
  6.7 3.4 %collective-permute-done = f32[12,8,128]{2,1,0:T(8,128)S(1)} collective-permute-done((f32[12,8,128]{2,1,0:T(8,128)}, f32[12,8,128]{2,1,0:T(8,128)S(1)}, u32[]{:S(2)}, u32[]{:S(2)}) %collective-permute-start) | collective-permute-done | bytes 49184 | tf_op jit(solution)/shard_map/ppermute | solution.py:393
  10.1 0.9 %pad_maximum_fusion.g0 = f32[57,8,128]{2,1,0:T(8,128)S(1)} fusion(f32[12,8,128]{2,1,0:T(8,128)S(1)} %fusion.2, f32[45,8,128]{2,1,0:T(8,128)} %get-tuple-element.4), kind=kLoop, calls=%fused_computation | loop fusion | flops 58368 | bytes 466944 | tf_op jit(solution)/shard_map/concatenate | solution.py:397
  11.1 4.1 %collective-permute-start.5 = (f32[57,8,128]{2,1,0:T(8,128)S(1)}, f32[57,8,128]{2,1,0:T(8,128)S(1)}, u32[]{:S(2)}, u32[]{:S(2)}) collective-permute-start(f32[57,8,128]{2,1,0:T(8,128)S(1)} %pad_maximum_fusion.g0), channel_id=1, source_target_pairs={{32,0},{48,16},{64,32},{80,48},{96,64},{112,80},{128,96},{144,112}... | collective-permute-start | bytes 700424 | tf_op jit(solution)/shard_map/ppermute | solution.py:398
  15.2 2.2 %collective-permute-start.4 = (f32[57,8,128]{2,1,0:T(8,128)S(1)}, f32[57,8,128]{2,1,0:T(8,128)S(1)}, u32[]{:S(2)}, u32[]{:S(2)}) collective-permute-start(f32[57,8,128]{2,1,0:T(8,128)S(1)} %pad_maximum_fusion.g0), channel_id=1, source_target_pairs={{16,0},{32,16},{48,32},{64,48},{80,64},{96,80},{112,96},{128,112},... | collective-permute-start | bytes 700424 | tf_op jit(solution)/shard_map/ppermute | solution.py:398
  17.5 6.0 %collective-permute-start.3 = (f32[57,8,128]{2,1,0:T(8,128)S(1)}, f32[57,8,128]{2,1,0:T(8,128)S(1)}, u32[]{:S(2)}, u32[]{:S(2)}) collective-permute-start(f32[57,8,128]{2,1,0:T(8,128)S(1)} %pad_maximum_fusion.g0), channel_id=1, source_target_pairs={{0,16},{16,32},{32,48},{48,64},{64,80},{80,96},{96,112},{112,128},... | collective-permute-start | bytes 700424 | tf_op jit(solution)/shard_map/ppermute | solution.py:398
  23.5 1.9 %collective-permute-start.2 = (f32[57,8,128]{2,1,0:T(8,128)S(1)}, f32[57,8,128]{2,1,0:T(8,128)S(1)}, u32[]{:S(2)}, u32[]{:S(2)}) collective-permute-start(f32[57,8,128]{2,1,0:T(8,128)S(1)} %pad_maximum_fusion.g0), channel_id=1, source_target_pairs={{0,32},{16,48},{32,64},{48,80},{64,96},{80,112},{96,128},{112,144}... | collective-permute-start | bytes 700424 | tf_op jit(solution)/shard_map/ppermute | solution.py:398
  25.4 0.1 fusion.1
  25.5 0.0 collective-permute-done.5.gp2
  25.5 2.6 %collective-permute-done.4.gp1 = f32[57,8,128]{2,1,0:T(8,128)S(1)} collective-permute-done((f32[57,8,128]{2,1,0:T(8,128)S(1)}, f32[57,8,128]{2,1,0:T(8,128)S(1)}, u32[]{:S(2)}, u32[]{:S(2)}) %collective-permute-start.4) | collective-permute-done | bytes 233504 | tf_op jit(solution)/shard_map/ppermute | solution.py:398
  28.1 4.9 %collective-permute-done.3.gm1 = f32[57,8,128]{2,1,0:T(8,128)S(1)} collective-permute-done((f32[57,8,128]{2,1,0:T(8,128)S(1)}, f32[57,8,128]{2,1,0:T(8,128)S(1)}, u32[]{:S(2)}, u32[]{:S(2)}) %collective-permute-start.3) | collective-permute-done | bytes 233504 | tf_op jit(solution)/shard_map/ppermute | solution.py:398
  33.0 3.9 %collective-permute-done.2.gm2 = f32[57,8,128]{2,1,0:T(8,128)S(1)} collective-permute-done((f32[57,8,128]{2,1,0:T(8,128)S(1)}, f32[57,8,128]{2,1,0:T(8,128)S(1)}, u32[]{:S(2)}, u32[]{:S(2)}) %collective-permute-start.2) | collective-permute-done | bytes 233504 | tf_op jit(solution)/shard_map/ppermute | solution.py:398
  36.9 30.2 %cycle.1 = (f32[2,20,8,128]{3,2,1,0:T(8,128)}, f32[2,20,8,128]{3,2,1,0:T(8,128)}) custom-call(f32[57,8,128]{2,1,0:T(8,128)S(1)} %collective-permute-done.2.gm2, f32[57,8,128]{2,1,0:T(8,128)S(1)} %collective-permute-done.3.gm1, f32[57,8,128]{2,1,0:T(8,128)S(1)} %pad_maximum_fusion.g0, f32[57,8,128]{2,1,0:T(8,128)S(1)} %collective-permute-done.4.gp1, ...), custom_call_target="tpu_custom_call" | custom-call | tf_op jit(solution)/shard_map/cycle/pallas_call | solution.py:403
  (5 shorter events, 0.0 us)
Async XLA Ops:
  2.3 4.4 %collective-permute-start.1 = (f32[12,8,128]{2,1,0:T(8,128)}, f32[12,8,128]{2,1,0:T(8,128)S(1)}, u32[]{:S(2)}, u32[]{:S(2)}) collective-permute-start(f32[12,8,128]{2,1,0:T(8,128)} %get-tuple-element.5), channel_id=1, source_target_pairs={{1,0},{2,1},{3,2},{4,3},{5,4},{6,5},{7,6},{8,7},{9,8},{10,9},{11,1... | collective-permute-start | bytes 147464 | tf_op jit(solution)/shard_map/ppermute | solution.py:394
  4.5 5.6 %collective-permute-start = (f32[12,8,128]{2,1,0:T(8,128)}, f32[12,8,128]{2,1,0:T(8,128)S(1)}, u32[]{:S(2)}, u32[]{:S(2)}) collective-permute-start(f32[12,8,128]{2,1,0:T(8,128)} %get-tuple-element.5), channel_id=1, source_target_pairs={{0,1},{1,2},{2,3},{3,4},{4,5},{5,6},{6,7},{7,8},{8,9},{9,10},{10,1... | collective-permute-start | bytes 147464 | tf_op jit(solution)/shard_map/ppermute | solution.py:393
  11.1 14.4 %collective-permute-start.5 = (f32[57,8,128]{2,1,0:T(8,128)S(1)}, f32[57,8,128]{2,1,0:T(8,128)S(1)}, u32[]{:S(2)}, u32[]{:S(2)}) collective-permute-start(f32[57,8,128]{2,1,0:T(8,128)S(1)} %pad_maximum_fusion.g0), channel_id=1, source_target_pairs={{32,0},{48,16},{64,32},{80,48},{96,64},{112,80},{128,96},{144,112}... | collective-permute-start | bytes 700424 | tf_op jit(solution)/shard_map/ppermute | solution.py:398
  15.2 12.9 %collective-permute-start.4 = (f32[57,8,128]{2,1,0:T(8,128)S(1)}, f32[57,8,128]{2,1,0:T(8,128)S(1)}, u32[]{:S(2)}, u32[]{:S(2)}) collective-permute-start(f32[57,8,128]{2,1,0:T(8,128)S(1)} %pad_maximum_fusion.g0), channel_id=1, source_target_pairs={{16,0},{32,16},{48,32},{64,48},{80,64},{96,80},{112,96},{128,112},... | collective-permute-start | bytes 700424 | tf_op jit(solution)/shard_map/ppermute | solution.py:398
  17.5 15.6 %collective-permute-start.3 = (f32[57,8,128]{2,1,0:T(8,128)S(1)}, f32[57,8,128]{2,1,0:T(8,128)S(1)}, u32[]{:S(2)}, u32[]{:S(2)}) collective-permute-start(f32[57,8,128]{2,1,0:T(8,128)S(1)} %pad_maximum_fusion.g0), channel_id=1, source_target_pairs={{0,16},{16,32},{32,48},{48,64},{64,80},{80,96},{96,112},{112,128},... | collective-permute-start | bytes 700424 | tf_op jit(solution)/shard_map/ppermute | solution.py:398
  23.5 13.4 %collective-permute-start.2 = (f32[57,8,128]{2,1,0:T(8,128)S(1)}, f32[57,8,128]{2,1,0:T(8,128)S(1)}, u32[]{:S(2)}, u32[]{:S(2)}) collective-permute-start(f32[57,8,128]{2,1,0:T(8,128)S(1)} %pad_maximum_fusion.g0), channel_id=1, source_target_pairs={{0,32},{16,48},{32,64},{48,80},{64,96},{80,112},{96,128},{112,144}... | collective-permute-start | bytes 700424 | tf_op jit(solution)/shard_map/ppermute | solution.py:398

commit v2 on v1

--- a/solution.py
+++ b/solution.py
@@ -9,6 +9,7 @@
 PLANES = 45
 STRIPS = 12
 F32 = jnp.float32
+UNROLL = 20
 
 
 def iotas(shape=(8, 128)):
@@ -127,7 +128,7 @@
                     E[z, lt, rows(k), :] = q * q
         return 0
 
-    lax.fori_loop(0, L, visc, 0)
+    lax.fori_loop(0, L, visc, 0, unroll=UNROLL)
 
     def factor(z, carry):
         top = jnp.where(z < L - 1, 1.0, 0.0)
@@ -159,7 +160,7 @@
         return tuple(out)
 
     zero = jnp.zeros((8, 128), F32)
-    lax.fori_loop(0, L, factor, (zero,) * 24)
+    lax.fori_loop(0, L, factor, (zero,) * 24, unroll=UNROLL)
 
     def forward(src, tiles, rim_tile):
         n = len(tiles)
@@ -180,7 +181,7 @@
                         out.append(C[p, lt, rows(k), :] * t)
             return tuple(out)
 
-        lax.fori_loop(0, L, step, (zero,) * (4 * n))
+        lax.fori_loop(0, L, step, (zero,) * (4 * n), unroll=UNROLL)
 
     def backward(src, dst, tiles):
         n = len(tiles)
@@ -197,7 +198,7 @@
                         out.append(new)
             return tuple(out)
 
-        lax.fori_loop(0, L, step, (zero,) * (4 * n))
+        lax.fori_loop(0, L, step, (zero,) * (4 * n), unroll=UNROLL)
 
     def remainder(src, tiles, put):
         n = len(tiles)
@@ -223,7 +224,7 @@
                 put(component, z, got)
             return tuple(out)
 
-        lax.fori_loop(0, L, step, (zero,) * (4 * n))
+        lax.fori_loop(0, L, step, (zero,) * (4 * n), unroll=UNROLL)
 
     pre = [0, 1, 2, 3]
     forward(V, pre, 4)
@@ -245,14 +246,14 @@
             CA[lt, pl.ds(pl.multiple_of(p * 16, 16), 16), :] = T[p, lt, even, :] + T[p, lt, odd, :]
         return 0
 
-    lax.fori_loop(0, 40, gather, 0)
+    lax.fori_loop(0, 40, gather, 0, unroll=UNROLL)
 
     def gather_eta(z, _):
         for lt in range(2):
             CA[lt, pl.ds(pl.multiple_of((z + 40) * 16, 16), 16), :] = E[z, lt, even, :] + E[z, lt, odd, :]
         return 0
 
-    lax.fori_loop(0, L, gather_eta, 0)
+    lax.fori_loop(0, L, gather_eta, 0, unroll=UNROLL)
     for i in range(3):
         for lt in range(2):
             CA[lt, (60 + i) * 16 : (61 + i) * 16, :] = F[2 + i, lt, even, :] + F[2 + i, lt, odd, :]
@@ -292,7 +293,7 @@
             out += new
         return tuple(out)
 
-    lax.fori_loop(0, L, coarse_factor, (zero,) * 6)
+    lax.fori_loop(0, L, coarse_factor, (zero,) * 6, unroll=UNROLL)
 
     for turn in range(4):
 
@@ -312,7 +313,7 @@
                     out.append(CC[at(p, k), :] * t)
             return tuple(out)
 
-        lax.fori_loop(0, L, coarse_forward, (zero,) * 4)
+        lax.fori_loop(0, L, coarse_forward, (zero,) * 4, unroll=UNROLL)
 
         def coarse_backward(s, carry, turn=turn):
             z = L - 1 - s
@@ -328,7 +329,7 @@
                     out.append(new)
             return tuple(out)
 
-        lax.fori_loop(0, L, coarse_backward, (zero,) * 4)
+        lax.fori_loop(0, L, coarse_backward, (zero,) * 4, unroll=UNROLL)
 
     def spread(p, _):
         CE[pl.ds(pl.multiple_of(p * 8, 8), 8), :] = pltpu.roll(
@@ -336,7 +337,7 @@
         )
         return 0
 
-    lax.fori_loop(0, 40, spread, 0)
+    lax.fori_loop(0, 40, spread, 0, unroll=UNROLL)
     for lt in range(2):
         CF[lt] = jnp.dot(CE[...], expand[lt], precision=lax.Precision.HIGHEST, preferred_element_type=F32)
 
@@ -350,7 +351,7 @@
                 X[p, lt, rows(k), :] = X[p, lt, rows(k), :] + m * PC[p, lt, rows(k - 1), :]
         return 0
 
-    lax.fori_loop(0, 40, correct, 0)
+    lax.fori_loop(0, 40, correct, 0, unroll=UNROLL)
 
     post = [1, 2]
     for _ in range(2):

time: 67.4 us -> 47.3 us (0.70)
  Pallas kernels: 31.9 us -> 11.9 us
    pallas_call x1, Pallas kernels: 30.2 us -> 10.2 us  [per_device(): pl.pallas_call(main_kernel, out_shape=(out, out), in_specs=[vmem] * 7, ou...]
where the time goes in v2:
time: 47.3 us; the launch traced here: 47 us
  starting transfers between devices  18.6 us (39%)
  waiting for transfers between devices  14.8 us (31%)
  Pallas kernels  11.9 us (25%)
  other arithmetic  1.08 us (2%)
  between operations  0.74 us (2%)
    ppermute x4, starting transfers between devices, per_device(): lax.ppermute(whole, 'gx', shift('gx', -by))  14.3 us
    ppermute x4, waiting for transfers between devices, per_device(): lax.ppermute(whole, 'gx', shift('gx', -by))  11.3 us
    pallas_call x1, Pallas kernels, per_device(): pl.pallas_call(main_kernel, out_shape=(out, out), in_specs=[vmem] * 7, ou...  10.2 us
    ppermute x1, waiting for transfers between devices, per_device(): left = lax.ppermute(strips, 'gy', shift('gy', 1))  3.41 us
    ppermute x1, starting transfers between devices, per_device(): right = lax.ppermute(strips, 'gy', shift('gy', -1))  2.16 us
    ppermute x1, starting transfers between devices, per_device(): left = lax.ppermute(strips, 'gy', shift('gy', 1))  2.15 us
    pallas_call x1, Pallas kernels, per_device(): pl.pallas_call(pack_kernel, out_shape=(jax.ShapeDtypeStruct((PLANES, 8, 1...  1.71 us
  transfers between devices with their start and end apart: 6, of which 4 were waited for; matrix products, arithmetic and copies ran while one was open for 0% of the time, Pallas kernels for 0%

profile of v2, /device:TPU:406, one launch (start us, length us, event | category | flops | bytes accessed | tf_op | source)
XLA Modules:
  0.0 47.0 jit_solution(4671593795627841283)
XLA Ops:
  0.6 1.7 %pack.1 = (f32[45,8,128]{2,1,0:T(8,128)}, f32[12,8,128]{2,1,0:T(8,128)}) custom-call(f32[2,20,8,128]{3,2,1,0:T(8,128)} %vel.1, f32[2,8,128]{2,1,0:T(8,128)} %drive.1, f32[8,128]{1,0:T(8,128)} %stiff.1, f32[8,128]{1,0:T(8,128)} %thick.1, s32[8,128]{1,0:T(8,128)} %ice.1, s32[8,128]{1,0:T(8,128)} %cls.1, f32[8]{0:T(128)} %table.1), custom_call_target="tpu_custom_call" | custom-call | tf_op jit(solution)/shard_map/pack/pallas_call | solution.py:387
  2.3 2.2 %collective-permute-start.1 = (f32[12,8,128]{2,1,0:T(8,128)}, f32[12,8,128]{2,1,0:T(8,128)S(1)}, u32[]{:S(2)}, u32[]{:S(2)}) collective-permute-start(f32[12,8,128]{2,1,0:T(8,128)} %get-tuple-element.5), channel_id=1, source_target_pairs={{1,0},{2,1},{3,2},{4,3},{5,4},{6,5},{7,6},{8,7},{9,8},{10,9},{11,1... | collective-permute-start | bytes 147464 | tf_op jit(solution)/shard_map/ppermute | solution.py:395
  4.5 2.1 %collective-permute-start = (f32[12,8,128]{2,1,0:T(8,128)}, f32[12,8,128]{2,1,0:T(8,128)S(1)}, u32[]{:S(2)}, u32[]{:S(2)}) collective-permute-start(f32[12,8,128]{2,1,0:T(8,128)} %get-tuple-element.5), channel_id=1, source_target_pairs={{0,1},{1,2},{2,3},{3,4},{4,5},{5,6},{6,7},{7,8},{8,9},{9,10},{10,1... | collective-permute-start | bytes 147464 | tf_op jit(solution)/shard_map/ppermute | solution.py:394
  6.7 0.0 collective-permute-done.1
  6.7 3.4 %collective-permute-done = f32[12,8,128]{2,1,0:T(8,128)S(1)} collective-permute-done((f32[12,8,128]{2,1,0:T(8,128)}, f32[12,8,128]{2,1,0:T(8,128)S(1)}, u32[]{:S(2)}, u32[]{:S(2)}) %collective-permute-start) | collective-permute-done | bytes 49184 | tf_op jit(solution)/shard_map/ppermute | solution.py:394
  10.1 0.9 %pad_maximum_fusion.g0 = f32[57,8,128]{2,1,0:T(8,128)S(1)} fusion(f32[12,8,128]{2,1,0:T(8,128)S(1)} %fusion.2, f32[45,8,128]{2,1,0:T(8,128)} %get-tuple-element.4), kind=kLoop, calls=%fused_computation | loop fusion | flops 58368 | bytes 466944 | tf_op jit(solution)/shard_map/concatenate | solution.py:398
  11.1 4.1 %collective-permute-start.5 = (f32[57,8,128]{2,1,0:T(8,128)S(1)}, f32[57,8,128]{2,1,0:T(8,128)S(1)}, u32[]{:S(2)}, u32[]{:S(2)}) collective-permute-start(f32[57,8,128]{2,1,0:T(8,128)S(1)} %pad_maximum_fusion.g0), channel_id=1, source_target_pairs={{32,0},{48,16},{64,32},{80,48},{96,64},{112,80},{128,96},{144,112}... | collective-permute-start | bytes 700424 | tf_op jit(solution)/shard_map/ppermute | solution.py:399
  15.2 2.2 %collective-permute-start.4 = (f32[57,8,128]{2,1,0:T(8,128)S(1)}, f32[57,8,128]{2,1,0:T(8,128)S(1)}, u32[]{:S(2)}, u32[]{:S(2)}) collective-permute-start(f32[57,8,128]{2,1,0:T(8,128)S(1)} %pad_maximum_fusion.g0), channel_id=1, source_target_pairs={{16,0},{32,16},{48,32},{64,48},{80,64},{96,80},{112,96},{128,112},... | collective-permute-start | bytes 700424 | tf_op jit(solution)/shard_map/ppermute | solution.py:399
  17.5 6.0 %collective-permute-start.3 = (f32[57,8,128]{2,1,0:T(8,128)S(1)}, f32[57,8,128]{2,1,0:T(8,128)S(1)}, u32[]{:S(2)}, u32[]{:S(2)}) collective-permute-start(f32[57,8,128]{2,1,0:T(8,128)S(1)} %pad_maximum_fusion.g0), channel_id=1, source_target_pairs={{0,16},{16,32},{32,48},{48,64},{64,80},{80,96},{96,112},{112,128},... | collective-permute-start | bytes 700424 | tf_op jit(solution)/shard_map/ppermute | solution.py:399
  23.5 1.9 %collective-permute-start.2 = (f32[57,8,128]{2,1,0:T(8,128)S(1)}, f32[57,8,128]{2,1,0:T(8,128)S(1)}, u32[]{:S(2)}, u32[]{:S(2)}) collective-permute-start(f32[57,8,128]{2,1,0:T(8,128)S(1)} %pad_maximum_fusion.g0), channel_id=1, source_target_pairs={{0,32},{16,48},{32,64},{48,80},{64,96},{80,112},{96,128},{112,144}... | collective-permute-start | bytes 700424 | tf_op jit(solution)/shard_map/ppermute | solution.py:399
  25.4 0.1 fusion.1
  25.5 0.0 collective-permute-done.5.gp2
  25.5 2.6 %collective-permute-done.4.gp1 = f32[57,8,128]{2,1,0:T(8,128)S(1)} collective-permute-done((f32[57,8,128]{2,1,0:T(8,128)S(1)}, f32[57,8,128]{2,1,0:T(8,128)S(1)}, u32[]{:S(2)}, u32[]{:S(2)}) %collective-permute-start.4) | collective-permute-done | bytes 233504 | tf_op jit(solution)/shard_map/ppermute | solution.py:399
  28.1 4.9 %collective-permute-done.3.gm1 = f32[57,8,128]{2,1,0:T(8,128)S(1)} collective-permute-done((f32[57,8,128]{2,1,0:T(8,128)S(1)}, f32[57,8,128]{2,1,0:T(8,128)S(1)}, u32[]{:S(2)}, u32[]{:S(2)}) %collective-permute-start.3) | collective-permute-done | bytes 233504 | tf_op jit(solution)/shard_map/ppermute | solution.py:399
  33.0 3.9 %collective-permute-done.2.gm2 = f32[57,8,128]{2,1,0:T(8,128)S(1)} collective-permute-done((f32[57,8,128]{2,1,0:T(8,128)S(1)}, f32[57,8,128]{2,1,0:T(8,128)S(1)}, u32[]{:S(2)}, u32[]{:S(2)}) %collective-permute-start.2) | collective-permute-done | bytes 233504 | tf_op jit(solution)/shard_map/ppermute | solution.py:399
  36.9 10.2 %cycle.1 = (f32[2,20,8,128]{3,2,1,0:T(8,128)}, f32[2,20,8,128]{3,2,1,0:T(8,128)}) custom-call(f32[57,8,128]{2,1,0:T(8,128)S(1)} %collective-permute-done.2.gm2, f32[57,8,128]{2,1,0:T(8,128)S(1)} %collective-permute-done.3.gm1, f32[57,8,128]{2,1,0:T(8,128)S(1)} %pad_maximum_fusion.g0, f32[57,8,128]{2,1,0:T(8,128)S(1)} %collective-permute-done.4.gp1, ...), custom_call_target="tpu_custom_call" | custom-call | tf_op jit(solution)/shard_map/cycle/pallas_call | solution.py:404
  (5 shorter events, 0.0 us)
Async XLA Ops:
  2.3 4.4 %collective-permute-start.1 = (f32[12,8,128]{2,1,0:T(8,128)}, f32[12,8,128]{2,1,0:T(8,128)S(1)}, u32[]{:S(2)}, u32[]{:S(2)}) collective-permute-start(f32[12,8,128]{2,1,0:T(8,128)} %get-tuple-element.5), channel_id=1, source_target_pairs={{1,0},{2,1},{3,2},{4,3},{5,4},{6,5},{7,6},{8,7},{9,8},{10,9},{11,1... | collective-permute-start | bytes 147464 | tf_op jit(solution)/shard_map/ppermute | solution.py:395
  4.5 5.6 %collective-permute-start = (f32[12,8,128]{2,1,0:T(8,128)}, f32[12,8,128]{2,1,0:T(8,128)S(1)}, u32[]{:S(2)}, u32[]{:S(2)}) collective-permute-start(f32[12,8,128]{2,1,0:T(8,128)} %get-tuple-element.5), channel_id=1, source_target_pairs={{0,1},{1,2},{2,3},{3,4},{4,5},{5,6},{6,7},{7,8},{8,9},{9,10},{10,1... | collective-permute-start | bytes 147464 | tf_op jit(solution)/shard_map/ppermute | solution.py:394
  11.1 14.4 %collective-permute-start.5 = (f32[57,8,128]{2,1,0:T(8,128)S(1)}, f32[57,8,128]{2,1,0:T(8,128)S(1)}, u32[]{:S(2)}, u32[]{:S(2)}) collective-permute-start(f32[57,8,128]{2,1,0:T(8,128)S(1)} %pad_maximum_fusion.g0), channel_id=1, source_target_pairs={{32,0},{48,16},{64,32},{80,48},{96,64},{112,80},{128,96},{144,112}... | collective-permute-start | bytes 700424 | tf_op jit(solution)/shard_map/ppermute | solution.py:399
  15.2 12.9 %collective-permute-start.4 = (f32[57,8,128]{2,1,0:T(8,128)S(1)}, f32[57,8,128]{2,1,0:T(8,128)S(1)}, u32[]{:S(2)}, u32[]{:S(2)}) collective-permute-start(f32[57,8,128]{2,1,0:T(8,128)S(1)} %pad_maximum_fusion.g0), channel_id=1, source_target_pairs={{16,0},{32,16},{48,32},{64,48},{80,64},{96,80},{112,96},{128,112},... | collective-permute-start | bytes 700424 | tf_op jit(solution)/shard_map/ppermute | solution.py:399
  17.5 15.6 %collective-permute-start.3 = (f32[57,8,128]{2,1,0:T(8,128)S(1)}, f32[57,8,128]{2,1,0:T(8,128)S(1)}, u32[]{:S(2)}, u32[]{:S(2)}) collective-permute-start(f32[57,8,128]{2,1,0:T(8,128)S(1)} %pad_maximum_fusion.g0), channel_id=1, source_target_pairs={{0,16},{16,32},{32,48},{48,64},{64,80},{80,96},{96,112},{112,128},... | collective-permute-start | bytes 700424 | tf_op jit(solution)/shard_map/ppermute | solution.py:399
  23.5 13.4 %collective-permute-start.2 = (f32[57,8,128]{2,1,0:T(8,128)S(1)}, f32[57,8,128]{2,1,0:T(8,128)S(1)}, u32[]{:S(2)}, u32[]{:S(2)}) collective-permute-start(f32[57,8,128]{2,1,0:T(8,128)S(1)} %pad_maximum_fusion.g0), channel_id=1, source_target_pairs={{0,32},{16,48},{32,64},{48,80},{64,96},{80,112},{96,128},{112,144}... | collective-permute-start | bytes 700424 | tf_op jit(solution)/shard_map/ppermute | solution.py:399

commit v3 on v2

--- a/solution.py
+++ b/solution.py
@@ -70,20 +70,25 @@
 
 
 def main_kernel(
-    gm2, gm1, g0, gp1, gp2, restrict, expand, vel_out, res_out,
+    parity, gm2, swap_b, g0, swap_a, gp2, restrict, expand, vel_out, res_out,
     V, F, Q, E, W, D, C, I, T, X, CA, CB, CE, CF, CX, CQ, CW, CC, CI, CT, PC,
 ):
     sub, lane = iotas()
     low = sub < 4
-    G = [gm2, gm1, g0, gp1, gp2]
+    odd = parity[0] == 1
     inner = (lane < 16) | (lane >= 112)
 
+    def from_all(p):
+        a, b = swap_a[p], swap_b[p]
+        return gm2[p], jnp.where(odd, a, b), g0[p], jnp.where(odd, b, a), gp2[p]
+
+    rims = [from_all(PLANES + j) for j in range(STRIPS)]
     for p in range(PLANES):
+        whole = from_all(p)
+        j, g = p // 4, p % 4
         for k in range(5):
-            a, b = G[k], G[(k + 1) % 5]
-            main = jnp.where(low, a[p], b[p])
-            j, g = PLANES + p // 4, p % 4
-            rim = jnp.where(low, a[j], b[j])
+            main = jnp.where(low, whole[k], whole[(k + 1) % 5])
+            rim = jnp.where(low, rims[j][k], rims[j][(k + 1) % 5])
             rim = pltpu.roll(rim, 128 - (32 * g + 16), 1)
             rim = jnp.where(inner, rim, 0.0)
             for lt, tile in ((0, main), (1, rim)):
@@ -376,9 +381,28 @@
     return restrict, expand
 
 
-def shift(axis, by):
-    count = lax.axis_size(axis)
-    return [(i, i + by) for i in range(count) if 0 <= i + by < count]
+def pairs(move):
+    def of(axis):
+        rows, cols = lax.axis_size("gx"), lax.axis_size("gy")
+        count = rows if axis == "gx" else cols
+        hops = [(i, move(i)) for i in range(count) if 0 <= move(i) < count]
+        if axis == "gx":
+            return [(i * cols + j, k * cols + j) for i, k in hops for j in range(cols)]
+        return [(i * cols + j, i * cols + k) for i in range(rows) for j, k in hops]
+
+    return of
+
+
+def send(cells, axis, move):
+    return lax.ppermute(cells, ("gx", "gy"), pairs(move)(axis))
+
+
+def inner_swap(i):
+    return i ^ 1
+
+
+def outer_swap(i):
+    return ((i + 1) ^ 1) - 1
 
 
 def per_device(velocity, drive, stiffness, thickness, ice_mask, friction_class, friction_table):
@@ -391,12 +415,20 @@
         out_specs=(vmem, vmem),
         name="pack",
     )(velocity, drive, stiffness, thickness, ice_mask, friction_class, friction_table)
-    left = lax.ppermute(strips, "gy", shift("gy", 1))
-    right = lax.ppermute(strips, "gy", shift("gy", -1))
+    inner = send(strips, "gy", inner_swap)
+    outer = send(strips, "gy", outer_swap)
+    odd = lax.axis_index("gy") % 2 == 1
+    left = jnp.where(odd, inner, outer)
+    right = jnp.where(odd, outer, inner)
     lane = lax.broadcasted_iota(jnp.int32, strips.shape, 2)
     rim = jnp.where(lane % 32 < 16, left, right)
     whole = jnp.concatenate([main, rim], axis=0)
-    parts = [whole if by == 0 else lax.ppermute(whole, "gx", shift("gx", -by)) for by in (-2, -1, 0, 1, 2)]
+    before = send(whole, "gx", lambda i: i + 2)
+    after = send(whole, "gx", lambda i: i - 2)
+    outer = send(whole, "gx", outer_swap)
+    inner = send(whole, "gx", inner_swap)
+    parity = (lax.axis_index("gx") % 2).astype(jnp.int32).reshape(1)
+    parts = (parity, before, outer, whole, inner, after)
     restrict, expand = transfer_matrices()
     fine = lambda n, r: pltpu.VMEM((n, 2, r, 128), F32)
     coarse = lambda n: pltpu.VMEM((16 * n, 128), F32)
@@ -404,7 +436,7 @@
     return pl.pallas_call(
         main_kernel,
         out_shape=(out, out),
-        in_specs=[vmem] * 7,
+        in_specs=[smem] + [vmem] * 7,
         out_specs=(vmem, vmem),
         scratch_shapes=[
             fine(40, 40), fine(5, 40), fine(20, 40), fine(20, 32), fine(20, 32), fine(40, 32), fine(40, 32), fine(40, 32),

time: 47.3 us -> 44.8 us (0.947)
  the two profiles are of different devices: /device:TPU:406 before, /device:TPU:408 now
where the time goes in v3:
time: 44.8 us; the launch traced here: 44.6 us
  starting transfers between devices  20 us (45%)
  waiting for transfers between devices  11.9 us (27%)
  Pallas kernels  11.8 us (26%)
  between operations  0.77 us (2%)
    ppermute x6, starting transfers between devices, send(): return lax.ppermute(cells, ('gx', 'gy'), pairs(move)(axis))  20 us
    ppermute x6, waiting for transfers between devices, send(): return lax.ppermute(cells, ('gx', 'gy'), pairs(move)(axis))  11.9 us
    pallas_call x1, Pallas kernels, per_device(): pl.pallas_call(main_kernel, out_shape=(out, out), in_specs=[smem] + [vmem...  10.1 us
    pallas_call x1, Pallas kernels, per_device(): pl.pallas_call(pack_kernel, out_shape=(jax.ShapeDtypeStruct((PLANES, 8, 1...  1.71 us
  transfers between devices with their start and end apart: 6, of which 3 were waited for; matrix products, arithmetic and copies ran while one was open for 0% of the time, Pallas kernels for 0%

profile of v3, /device:TPU:408, one launch (start us, length us, event | category | flops | bytes accessed | tf_op | source)
XLA Modules:
  0.0 44.6 jit_solution(3834444582122391203)
XLA Ops:
  0.6 1.7 %pack.1 = (f32[45,8,128]{2,1,0:T(8,128)}, f32[12,8,128]{2,1,0:T(8,128)}) custom-call(f32[2,20,8,128]{3,2,1,0:T(8,128)} %vel.1, f32[2,8,128]{2,1,0:T(8,128)} %drive.1, f32[8,128]{1,0:T(8,128)} %stiff.1, f32[8,128]{1,0:T(8,128)} %thick.1, s32[8,128]{1,0:T(8,128)} %ice.1, s32[8,128]{1,0:T(8,128)} %cls.1, f32[8]{0:T(128)} %table.1), custom_call_target="tpu_custom_call" | custom-call | tf_op jit(solution)/shard_map/pack/pallas_call | solution.py:411
  2.3 0.0 copy-start
  2.3 4.4 %collective-permute-start.1 = (f32[12,8,128]{2,1,0:T(8,128)}, f32[12,8,128]{2,1,0:T(8,128)S(1)}, u32[]{:S(2)}, u32[]{:S(2)}) collective-permute-start(f32[12,8,128]{2,1,0:T(8,128)} %get-tuple-element.5), channel_id=1, source_target_pairs={{1,2},{2,1},{3,4},{4,3},{5,6},{6,5},{7,8},{8,7},{9,10},{10,9},{11,... | collective-permute-start | bytes 147464 | tf_op jit(solution)/shard_map/ppermute | solution.py:397
  6.8 1.9 %collective-permute-start = (f32[12,8,128]{2,1,0:T(8,128)}, f32[12,8,128]{2,1,0:T(8,128)S(1)}, u32[]{:S(2)}, u32[]{:S(2)}) collective-permute-start(f32[12,8,128]{2,1,0:T(8,128)} %get-tuple-element.5), channel_id=1, source_target_pairs={{0,1},{1,0},{2,3},{3,2},{4,5},{5,4},{6,7},{7,6},{8,9},{9,8},{10,11... | collective-permute-start | bytes 147464 | tf_op jit(solution)/shard_map/ppermute | solution.py:397
  8.7 1.5 %collective-permute-done.1 = f32[12,8,128]{2,1,0:T(8,128)S(1)} collective-permute-done((f32[12,8,128]{2,1,0:T(8,128)}, f32[12,8,128]{2,1,0:T(8,128)S(1)}, u32[]{:S(2)}, u32[]{:S(2)}) %collective-permute-start.1) | collective-permute-done | bytes 49184 | tf_op jit(solution)/shard_map/ppermute | solution.py:397
  10.2 0.0 collective-permute-done
  10.2 0.0 copy-done
  10.2 4.1 %collective-permute-start.5 = (f32[57,8,128]{2,1,0:T(8,128)S(1)}, f32[57,8,128]{2,1,0:T(8,128)S(1)}, u32[]{:S(2)}, u32[]{:S(2)}) collective-permute-start(f32[57,8,128]{2,1,0:T(8,128)S(1)} %pad_maximum_fusion.g0), channel_id=1, source_target_pairs={{32,0},{33,1},{34,2},{35,3},{36,4},{37,5},{38,6},{39,7},{40,8},{41... | collective-permute-start | bytes 700424 | tf_op jit(solution)/shard_map/ppermute | solution.py:397
  14.4 3.1 %collective-permute-start.4 = (f32[57,8,128]{2,1,0:T(8,128)S(1)}, f32[57,8,128]{2,1,0:T(8,128)S(1)}, u32[]{:S(2)}, u32[]{:S(2)}) collective-permute-start(f32[57,8,128]{2,1,0:T(8,128)S(1)} %pad_maximum_fusion.g0), channel_id=1, source_target_pairs={{0,16},{1,17},{2,18},{3,19},{4,20},{5,21},{6,22},{7,23},{8,24},{9,... | collective-permute-start | bytes 700424 | tf_op jit(solution)/shard_map/ppermute | solution.py:397
  17.5 3.4 %collective-permute-start.3 = (f32[57,8,128]{2,1,0:T(8,128)S(1)}, f32[57,8,128]{2,1,0:T(8,128)S(1)}, u32[]{:S(2)}, u32[]{:S(2)}) collective-permute-start(f32[57,8,128]{2,1,0:T(8,128)S(1)} %pad_maximum_fusion.g0), channel_id=1, source_target_pairs={{16,32},{17,33},{18,34},{19,35},{20,36},{21,37},{22,38},{23,39},{2... | collective-permute-start | bytes 700424 | tf_op jit(solution)/shard_map/ppermute | solution.py:397
  21.0 2.9 %collective-permute-start.2 = (f32[57,8,128]{2,1,0:T(8,128)S(1)}, f32[57,8,128]{2,1,0:T(8,128)S(1)}, u32[]{:S(2)}, u32[]{:S(2)}) collective-permute-start(f32[57,8,128]{2,1,0:T(8,128)S(1)} %pad_maximum_fusion.g0), channel_id=1, source_target_pairs={{0,32},{1,33},{2,34},{3,35},{4,36},{5,37},{6,38},{7,39},{8,40},{9,... | collective-permute-start | bytes 700424 | tf_op jit(solution)/shard_map/ppermute | solution.py:397
  23.9 0.1 fusion.1
  24.1 0.0 collective-permute-done.5.gp2
  24.1 6.1 %collective-permute-done.4.swap_a = f32[57,8,128]{2,1,0:T(8,128)S(1)} collective-permute-done((f32[57,8,128]{2,1,0:T(8,128)S(1)}, f32[57,8,128]{2,1,0:T(8,128)S(1)}, u32[]{:S(2)}, u32[]{:S(2)}) %collective-permute-start.4) | collective-permute-done | bytes 233504 | tf_op jit(solution)/shard_map/ppermute | solution.py:397
  30.2 0.0 collective-permute-done.3.swap_b
  30.2 4.3 %collective-permute-done.2.gm2 = f32[57,8,128]{2,1,0:T(8,128)S(1)} collective-permute-done((f32[57,8,128]{2,1,0:T(8,128)S(1)}, f32[57,8,128]{2,1,0:T(8,128)S(1)}, u32[]{:S(2)}, u32[]{:S(2)}) %collective-permute-start.2) | collective-permute-done | bytes 233504 | tf_op jit(solution)/shard_map/ppermute | solution.py:397
  34.5 10.1 %cycle.1 = (f32[2,20,8,128]{3,2,1,0:T(8,128)}, f32[2,20,8,128]{3,2,1,0:T(8,128)}) custom-call(s32[1]{0:T(128)} %bitcast.parity, f32[57,8,128]{2,1,0:T(8,128)S(1)} %collective-permute-done.2.gm2, f32[57,8,128]{2,1,0:T(8,128)S(1)} %collective-permute-done.3.swap_b, f32[57,8,128]{2,1,0:T(8,128)S(1)} %pad_maximum_fusion.g0, ...), custom_call_target="tpu_custom_call" | custom-call | tf_op jit(solution)/shard_map/cycle/pallas_call | solution.py:436
  (6 shorter events, 0.1 us)
Async XLA Ops:
  2.3 7.9 %copy-start = (f32[45,8,128]{2,1,0:T(8,128)S(1)}, f32[45,8,128]{2,1,0:T(8,128)}, u32[]{:S(2)}) copy-start(f32[45,8,128]{2,1,0:T(8,128)} %get-tuple-element.4) | copy-start | bytes 552964
  2.3 7.8 %collective-permute-start.1 = (f32[12,8,128]{2,1,0:T(8,128)}, f32[12,8,128]{2,1,0:T(8,128)S(1)}, u32[]{:S(2)}, u32[]{:S(2)}) collective-permute-start(f32[12,8,128]{2,1,0:T(8,128)} %get-tuple-element.5), channel_id=1, source_target_pairs={{1,2},{2,1},{3,4},{4,3},{5,6},{6,5},{7,8},{8,7},{9,10},{10,9},{11,... | collective-permute-start | bytes 147464 | tf_op jit(solution)/shard_map/ppermute | solution.py:397
  6.8 3.4 %collective-permute-start = (f32[12,8,128]{2,1,0:T(8,128)}, f32[12,8,128]{2,1,0:T(8,128)S(1)}, u32[]{:S(2)}, u32[]{:S(2)}) collective-permute-start(f32[12,8,128]{2,1,0:T(8,128)} %get-tuple-element.5), channel_id=1, source_target_pairs={{0,1},{1,0},{2,3},{3,2},{4,5},{5,4},{6,7},{7,6},{8,9},{9,8},{10,11... | collective-permute-start | bytes 147464 | tf_op jit(solution)/shard_map/ppermute | solution.py:397
  10.2 13.8 %collective-permute-start.5 = (f32[57,8,128]{2,1,0:T(8,128)S(1)}, f32[57,8,128]{2,1,0:T(8,128)S(1)}, u32[]{:S(2)}, u32[]{:S(2)}) collective-permute-start(f32[57,8,128]{2,1,0:T(8,128)S(1)} %pad_maximum_fusion.g0), channel_id=1, source_target_pairs={{32,0},{33,1},{34,2},{35,3},{36,4},{37,5},{38,6},{39,7},{40,8},{41... | collective-permute-start | bytes 700424 | tf_op jit(solution)/shard_map/ppermute | solution.py:397
  14.4 15.8 %collective-permute-start.4 = (f32[57,8,128]{2,1,0:T(8,128)S(1)}, f32[57,8,128]{2,1,0:T(8,128)S(1)}, u32[]{:S(2)}, u32[]{:S(2)}) collective-permute-start(f32[57,8,128]{2,1,0:T(8,128)S(1)} %pad_maximum_fusion.g0), channel_id=1, source_target_pairs={{0,16},{1,17},{2,18},{3,19},{4,20},{5,21},{6,22},{7,23},{8,24},{9,... | collective-permute-start | bytes 700424 | tf_op jit(solution)/shard_map/ppermute | solution.py:397
  17.5 12.6 %collective-permute-start.3 = (f32[57,8,128]{2,1,0:T(8,128)S(1)}, f32[57,8,128]{2,1,0:T(8,128)S(1)}, u32[]{:S(2)}, u32[]{:S(2)}) collective-permute-start(f32[57,8,128]{2,1,0:T(8,128)S(1)} %pad_maximum_fusion.g0), channel_id=1, source_target_pairs={{16,32},{17,33},{18,34},{19,35},{20,36},{21,37},{22,38},{23,39},{2... | collective-permute-start | bytes 700424 | tf_op jit(solution)/shard_map/ppermute | solution.py:397
  21.0 13.5 %collective-permute-start.2 = (f32[57,8,128]{2,1,0:T(8,128)S(1)}, f32[57,8,128]{2,1,0:T(8,128)S(1)}, u32[]{:S(2)}, u32[]{:S(2)}) collective-permute-start(f32[57,8,128]{2,1,0:T(8,128)S(1)} %pad_maximum_fusion.g0), channel_id=1, source_target_pairs={{0,32},{1,33},{2,34},{3,35},{4,36},{5,37},{6,38},{7,39},{8,40},{9,... | collective-permute-start | bytes 700424 | tf_op jit(solution)/shard_map/ppermute | solution.py:397

commit v4 on v3

v4 whole, which is shorter than its diff:
```python
import jax
import jax.numpy as jnp
from jax import lax
from jax.experimental import pallas as pl
from jax.experimental.pallas import tpu as pltpu
from jax.sharding import PartitionSpec as P

L = 20
PLANES = 45
STRIPS = 12
F32 = jnp.float32
UNROLL = 20


def iotas(shape=(8, 128)):
    return lax.broadcasted_iota(jnp.int32, shape, 0), lax.broadcasted_iota(jnp.int32, shape, 1)


def pack_kernel(vel, drive, stiff, thick, ice, cls, table, main, strips):
    sub, lane = iotas()
    m = ice[...].astype(F32)
    drag = jnp.zeros((8, 128), F32)
    for i in range(8):
        drag = jnp.where(cls[...] == i, table[i], drag)

    def plane(p):
        if p < 40:
            return vel[p // L, p % L] * m
        return (drive[0] * m, drive[1] * m, 0.5 * stiff[...] * m, thick[...], drag * m)[p - 40]

    for j in range(STRIPS):
        packed = jnp.zeros((8, 128), F32)
        for g in range(4):
            p = 4 * j + g
            if p < PLANES:
                tile = pltpu.roll(plane(p), 4, 0)
                main[p] = tile
                moved = pltpu.roll(tile, (32 * g + 16) % 128, 1)
                packed = jnp.where((lane >= 32 * g) & (lane < 32 * g + 32), moved, packed)
        strips[j] = packed


def beside(tiles, lane):
    out = []
    for lt, row in enumerate(tiles):
        pairs_ = []
        for k, here in enumerate(row):
            other = tiles[lt - 1][k]
            before = here if len(tiles) == 1 else jnp.where(lane == 127, other, here)
            after = here if len(tiles) == 1 else jnp.where(lane == 0, other, here)
            pairs_.append((pltpu.roll(before, 1, 1), pltpu.roll(after, 127, 1)))
        out.append(pairs_)
    return out


def weighted(component, row_pair, col_pair):
    a = row_pair[0] + row_pair[1]
    b = col_pair[0] + col_pair[1]
    return 4.0 * a + b if component == 0 else a + 4.0 * b


def product(values, weights):
    first = values.astype(jnp.bfloat16)
    second = (values - first.astype(F32)).astype(jnp.bfloat16)
    return jnp.dot(jnp.concatenate([first, second], axis=1), weights, preferred_element_type=F32)


def main_kernel(
    parity, gm2, swap_b, g0, swap_a, gp2, restrict, expand, vel_out, res_out,
    V, F, Q, R, E, W, FS, D, C, I, T, X, CA, CB, CE, CF, CX, CQ, CR, CC, CI, CT, PC,
):
    sub, lane = iotas()
    low = sub < 4
    odd = parity[0] == 1
    inner = (lane < 16) | (lane >= 112)

    def from_all(p):
        a, b = swap_a[p], swap_b[p]
        return gm2[p], jnp.where(odd, a, b), g0[p], jnp.where(odd, b, a), gp2[p]

    rims = [from_all(PLANES + j) for j in range(STRIPS)]
    for p in range(PLANES):
        whole = from_all(p)
        j, g = p // 4, p % 4
        for k in range(5):
            main = jnp.where(low, whole[k], whole[(k + 1) % 5])
            rim = jnp.where(low, rims[j][k], rims[j][(k + 1) % 5])
            rim = pltpu.roll(rim, 128 - (32 * g + 16), 1)
            rim = jnp.where(inner, rim, 0.0)
            for lt, tile in ((0, main), (1, rim)):
                if p < 40:
                    V[p, lt, 8 * k + 8 : 8 * k + 16, :] = tile
                    if k == 4:
                        V[p, lt, 0:8, :] = tile
                    if k == 0:
                        V[p, lt, 48:56, :] = tile
                else:
                    if p == 43:
                        tile = jnp.where(tile > 0.0, tile, 1.0)
                    F[p - 40, lt, 8 * k : 8 * k + 8, :] = tile

    def rows(k):
        return slice(8 * k, 8 * k + 8)

    def inside(k):
        return slice(8 * k + 8, 8 * k + 16)

    def around(ref, p, tiles):
        here = [[ref[p, lt, inside(k), :] for k in tiles] for lt in range(2)]
        up_down = [[(ref[p, lt, pl.ds(8 * k + 7, 8), :], ref[p, lt, pl.ds(8 * k + 9, 8), :]) for k in tiles] for lt in range(2)]
        return here, up_down, beside(here, lane)

    root = [[jnp.sqrt(F[2, lt, rows(k), :]) for k in range(5)] for lt in range(2)]
    quarter = [[25.0 / (F[3, lt, rows(k), :] * F[3, lt, rows(k), :]) for k in range(5)] for lt in range(2)]
    for lt in range(2):
        for k in range(5):
            T[0, lt, rows(k), :] = root[lt][k]
            T[1, lt, rows(k), :] = quarter[lt][k]
            T[2, lt, rows(k), :] = jnp.where(root[lt][k] > 0.0, 1.0 / root[lt][k], 0.0)

    def visc(z, _):
        after, before = jnp.minimum(z + 1, L - 1), jnp.maximum(z - 1, 0)
        u, ur, uc = around(V, z, range(5))
        ux = [[ur[lt][k][1] - ur[lt][k][0] for k in range(5)] for lt in range(2)]
        uy = [[uc[lt][k][1] - uc[lt][k][0] for k in range(5)] for lt in range(2)]
        v, vr, vc = around(V, z + L, range(5))
        for lt in range(2):
            for k in range(5):
                vx = vr[lt][k][1] - vr[lt][k][0]
                vy = vc[lt][k][1] - vc[lt][k][0]
                uz = V[after, lt, inside(k), :] - V[before, lt, inside(k), :]
                vz = V[after + L, lt, inside(k), :] - V[before + L, lt, inside(k), :]
                x, y = ux[lt][k], uy[lt][k]
                shear = y + vx
                plane = x * x + vy * vy + x * vy + 0.25 * (shear * shear)
                eps = 0.25 * plane + T[1, lt, rows(k), :] * (uz * uz + vz * vz) + 0.01
                sixth = jnp.log(eps) * (1.0 / 6.0)
                q = T[0, lt, rows(k), :] * jnp.exp(-sixth)
                for place in (inside(k), slice(0, 8))[: 2 if k == 4 else 1]:
                    Q[z, lt, place, :] = q
                    X[z, lt, place, :] = q * u[lt][k]
                    X[z + L, lt, place, :] = q * v[lt][k]
                if k < 4:
                    back = T[2, lt, rows(k), :] * jnp.exp(sixth)
                    R[z, lt, rows(k), :] = back
                    E[z, lt, rows(k), :] = q * q
                    FS[z, lt, rows(k), :] = F[0, lt, rows(k), :] * back
                    FS[z + L, lt, rows(k), :] = F[1, lt, rows(k), :] * back
        return 0

    lax.fori_loop(0, L, visc, 0, unroll=UNROLL)

    def factor(z, carry):
        top = jnp.where(z < L - 1, 1.0, 0.0)
        bed = jnp.where(z == 0, 1.0, 0.0)
        after = jnp.minimum(z + 1, L - 1)
        q, qr, qc = around(Q, z, range(4))
        out = []
        for lt in range(2):
            for k in range(4):
                i = lt * 4 + k
                wbefore, sbefore, cx, cy = carry[4 * i : 4 * i + 4]
                ice = F[2, lt, rows(k), :] > 0.0
                ih = 20.0 / F[3, lt, rows(k), :]
                back = R[z, lt, rows(k), :]
                w = (E[z, lt, rows(k), :] + E[after, lt, rows(k), :]) * (0.5 * top * (ih * ih))
                scaled = w * (back * R[after, lt, rows(k), :])
                common = (w + wbefore + bed * (F[4, lt, rows(k), :] * ih)) * (back * back)
                off = jnp.where(ice, 0.0, 1.0)
                share = jnp.where(ice, 0.8, 0.0)
                W[z, lt, rows(k), :] = scaled
                new = [w, scaled]
                for component, cb in ((0, cx), (1, cy)):
                    d = back * weighted(component, qr[lt][k], qc[lt][k]) + common
                    inv = 1.0 / (d + off - sbefore * cb)
                    c = scaled * inv
                    D[component * L + z, lt, rows(k), :] = d
                    I[component * L + z, lt, rows(k), :] = share * inv
                    C[component * L + z, lt, rows(k), :] = c
                    new.append(c)
                out += new
        return tuple(out)

    zero = jnp.zeros((8, 128), F32)
    lax.fori_loop(0, L, factor, (zero,) * 32, unroll=UNROLL)

    def forward(tiles):
        n = len(tiles)

        def step(z, carry):
            out = []
            for component in range(2):
                p = component * L + z
                y, yr, yc = around(X, p, tiles)
                for lt in range(2):
                    for i, k in enumerate(tiles):
                        t = FS[p, lt, rows(k), :] + weighted(component, yr[lt][i], yc[lt][i])
                        t = t + carry[(component * 2 + lt) * n + i]
                        T[p, lt, rows(k), :] = t
                        out.append(C[p, lt, rows(k), :] * t)
            return tuple(out)

        lax.fori_loop(0, L, step, (zero,) * (4 * n), unroll=UNROLL)

    def backward(tiles):
        n = len(tiles)

        def step(s, carry):
            z = L - 1 - s
            out = []
            for component in range(2):
                p = component * L + z
                for lt in range(2):
                    for i, k in enumerate(tiles):
                        new = I[p, lt, rows(k), :] * T[p, lt, rows(k), :] + C[p, lt, rows(k), :] * carry[(component * 2 + lt) * n + i]
                        X[p, lt, inside(k), :] = 0.2 * X[p, lt, inside(k), :] + new
                        out.append(new)
            return tuple(out)

        lax.fori_loop(0, L, step, (zero,) * (4 * n), unroll=UNROLL)

    def remainder(tiles, put):
        n = len(tiles)

        def step(z, carry):
            after = jnp.minimum(z + 1, L - 1)
            out = []
            for component in range(2):
                p = component * L + z
                y, yr, yc = around(X, p, tiles)
                got = []
                for lt in range(2):
                    for i, k in enumerate(tiles):
                        w = W[z, lt, rows(k), :]
                        r = FS[p, lt, rows(k), :] + weighted(component, yr[lt][i], yc[lt][i])
                        r = r - D[p, lt, rows(k), :] * y[lt][i]
                        r = r + w * X[after + component * L, lt, inside(k), :] + carry[(component * 2 + lt) * n + i]
                        got.append(Q[z, lt, inside(k), :] * r)
                        out.append(w * y[lt][i])
                put(component, z, got)
            return tuple(out)

        lax.fori_loop(0, L, step, (zero,) * (4 * n), unroll=UNROLL)

    pre = [0, 1, 2, 3]
    forward(pre)
    backward(pre)
    forward(pre)
    backward(pre)

    def put_rem(component, z, got):
        for lt in range(2):
            for i, k in enumerate(pre):
                T[component * L + z, lt, rows(k), :] = got[lt * 4 + i]

    remainder(pre, put_rem)

    even, odd = pl.ds(0, 16, stride=2), pl.ds(1, 16, stride=2)

    def gather(p, _):
        for lt in range(2):
            CA[lt, pl.ds(pl.multiple_of(p * 16, 16), 16), :] = T[p, lt, even, :] + T[p, lt, odd, :]
        return 0

    lax.fori_loop(0, 40, gather, 0, unroll=UNROLL)

    def gather_eta(z, _):
        for lt in range(2):
            CA[lt, pl.ds(pl.multiple_of((z + 40) * 16, 16), 16), :] = E[z, lt, even, :] + E[z, lt, odd, :]
        return 0

    lax.fori_loop(0, L, gather_eta, 0, unroll=UNROLL)
    for i in range(3):
        for lt in range(2):
            CA[lt, (60 + i) * 16 : (61 + i) * 16, :] = F[2 + i, lt, even, :] + F[2 + i, lt, odd, :]
    CB[...] = product(CA[0], restrict[0]) + product(CA[1], restrict[1])

    cmask = [jnp.where(CB[960 + 8 * k : 968 + 8 * k, :] > 0.0, 0.0, 1.0) for k in range(2)]
    cthick = [CB[976 + 8 * k : 984 + 8 * k, :] for k in range(2)]
    cih = [20.0 / jnp.where(t > 0.0, t, 1.0) for t in cthick]
    cdrag = [CB[992 + 8 * k : 1000 + 8 * k, :] * cih[k] for k in range(2)]

    def padded(p, k, by=0):
        return pl.ds(p * 16 + 8 * k + 8 + by, 8)

    def coarse_around(ref, p):
        here = [ref[padded(p, k), :] for k in range(2)]
        up_down = [(ref[padded(p, k, -1), :], ref[padded(p, k, 1), :]) for k in range(2)]
        return up_down, beside([here], lane)[0]

    for ref, size in ((CX, 40), (CQ, 20)):
        ref[0:8, :] = zero
        ref[16 * size + 8 : 16 * size + 16, :] = zero

    def at(p, k):
        return pl.ds(pl.multiple_of(p * 16 + 8 * k, 8), 8)

    def coarse_roots(z, _):
        for k in range(2):
            e = CB[at(40 + z, k), :]
            q = 0.5 * jnp.sqrt(e)
            back = jnp.where(e > 0.0, 1.0 / q, 0.0)
            CQ[padded(z, k), :] = q
            CR[at(z, k), :] = back
            for component in range(2):
                CB[at(component * L + z, k), :] = CB[at(component * L + z, k), :] * back
        return 0

    lax.fori_loop(0, L, coarse_roots, 0, unroll=UNROLL)

    def coarse_factor(z, carry):
        top = jnp.where(z < L - 1, 1.0, 0.0)
        bed = jnp.where(z == 0, 1.0, 0.0)
        after = jnp.minimum(z + 1, L - 1)
        qr, qc = coarse_around(CQ, z)
        out = []
        for k in range(2):
            wbefore, sbefore, cx, cy = carry[4 * k : 4 * k + 4]
            back = CR[at(z, k), :]
            w = (CB[at(40 + z, k), :] + CB[at(40 + after, k), :]) * (0.5 * top * (cih[k] * cih[k]))
            scaled = w * (back * CR[at(after, k), :])
            common = (w + wbefore + bed * cdrag[k]) * (back * back)
            new = [w, scaled]
            for component, cb in ((0, cx), (1, cy)):
                d = back * weighted(component, qr[k], qc[k]) + common
                inv = 1.0 / (d + cmask[k] - sbefore * cb)
                c = scaled * inv
                CI[at(component * L + z, k), :] = (0.8 - 0.8 * cmask[k]) * inv
                CC[at(component * L + z, k), :] = c
                new.append(c)
            out += new
        return tuple(out)

    lax.fori_loop(0, L, coarse_factor, (zero,) * 8, unroll=UNROLL)

    for turn in range(4):

        def coarse_forward(z, carry, turn=turn):
            out = []
            for component in range(2):
                p = component * L + z
                if turn > 0:
                    yr, yc = coarse_around(CX, p)
                for k in range(2):
                    t = CB[at(p, k), :] + carry[component * 2 + k]
                    if turn > 0:
                        t = t + weighted(component, yr[k], yc[k])
                    CT[at(p, k), :] = t
                    out.append(CC[at(p, k), :] * t)
            return tuple(out)

        lax.fori_loop(0, L, coarse_forward, (zero,) * 4, unroll=UNROLL)

        def coarse_backward(s, carry, turn=turn):
            z = L - 1 - s
            out = []
            for component in range(2):
                p = component * L + z
                for k in range(2):
                    new = CI[at(p, k), :] * CT[at(p, k), :] + CC[at(p, k), :] * carry[component * 2 + k]
                    if turn > 0:
                        CX[padded(p, k), :] = 0.2 * CX[padded(p, k), :] + new
                    else:
                        CX[padded(p, k), :] = new
                    out.append(new)
            return tuple(out)

        lax.fori_loop(0, L, coarse_backward, (zero,) * 4, unroll=UNROLL)

    def spread(p, _):
        CE[pl.ds(pl.multiple_of(p * 8, 8), 8), :] = pltpu.roll(
            jnp.where(low, CX[padded(p, 1), :] * CR[at(lax.rem(p, L), 1), :], CX[padded(p, 0), :] * CR[at(lax.rem(p, L), 0), :]), 4, 0
        )
        return 0

    lax.fori_loop(0, 40, spread, 0, unroll=UNROLL)
    for lt in range(2):
        CF[lt] = product(CE[...], expand[lt])

    def correct(p, _):
        for lt in range(2):
            tile = CF[lt, pl.ds(pl.multiple_of(p * 8, 8), 8), :]
            PC[p, lt, pl.ds(0, 8, stride=2), :] = tile
            PC[p, lt, pl.ds(1, 8, stride=2), :] = tile
            for k in (1, 2):
                q = Q[lax.rem(p, L), lt, inside(k), :]
                X[p, lt, inside(k), :] = X[p, lt, inside(k), :] + q * PC[p, lt, rows(k - 1), :]
        return 0

    lax.fori_loop(0, 40, correct, 0, unroll=UNROLL)

    post = [1, 2]
    for _ in range(2):
        forward(post)
        backward(post)

    def put_res(component, z, got):
        res_out[component, z] = pltpu.roll(jnp.where(low, got[1], got[0]), 4, 0)
        p = component * L + z
        vel = [X[p, 0, inside(k), :] * R[z, 0, rows(k), :] for k in (1, 2)]
        vel_out[component, z] = pltpu.roll(jnp.where(low, vel[1], vel[0]), 4, 0)

    remainder(post, put_res)


def transfer_matrices():
    lane = jnp.arange(128)
    main = lane // 2
    rim = jnp.where(lane < 16, 64 + lane // 2, jnp.where(lane >= 112, 120 + (lane - 112) // 2, -1))
    hits = jnp.stack([main, rim])[:, :, None] == lane[None, None, :]
    restrict = jnp.where(hits, 0.25, 0.0).astype(F32)
    expand = jnp.where(hits, 1.0, 0.0).astype(F32).transpose(0, 2, 1)
    twice = lambda w: jnp.concatenate([w, w], axis=1).astype(jnp.bfloat16)
    return twice(restrict), twice(expand)


def pairs(move):
    def of(axis):
        rows, cols = lax.axis_size("gx"), lax.axis_size("gy")
        count = rows if axis == "gx" else cols
        hops = [(i, move(i)) for i in range(count) if 0 <= move(i) < count]
        if axis == "gx":
            return [(i * cols + j, k * cols + j) for i, k in hops for j in range(cols)]
        return [(i * cols + j, i * cols + k) for i in range(rows) for j, k in hops]

    return of


def send(cells, axis, move):
    return lax.ppermute(cells, ("gx", "gy"), pairs(move)(axis))


def inner_swap(i):
    return i ^ 1


def outer_swap(i):
    return ((i + 1) ^ 1) - 1


def per_device(velocity, drive, stiffness, thickness, ice_mask, friction_class, friction_table):
    vmem = pl.BlockSpec(memory_space=pltpu.VMEM)
    smem = pl.BlockSpec(memory_space=pltpu.SMEM)
    main, strips = pl.pallas_call(
        pack_kernel,
        out_shape=(jax.ShapeDtypeStruct((PLANES, 8, 128), F32), jax.ShapeDtypeStruct((STRIPS, 8, 128), F32)),
        in_specs=[vmem] * 6 + [smem],
        out_specs=(vmem, vmem),
        name="pack",
    )(velocity, drive, stiffness, thickness, ice_mask, friction_class, friction_table)
    inner = send(strips, "gy", inner_swap)
    outer = send(strips, "gy", outer_swap)
    odd = lax.axis_index("gy") % 2 == 1
    left = jnp.where(odd, inner, outer)
    right = jnp.where(odd, outer, inner)
    lane = lax.broadcasted_iota(jnp.int32, strips.shape, 2)
    rim = jnp.where(lane % 32 < 16, left, right)
    whole = jnp.concatenate([main, rim], axis=0)
    before = send(whole, "gx", lambda i: i + 2)
    after = send(whole, "gx", lambda i: i - 2)
    outer = send(whole, "gx", outer_swap)
    inner = send(whole, "gx", inner_swap)
    parity = (lax.axis_index("gx") % 2).astype(jnp.int32).reshape(1)
    parts = (parity, before, outer, whole, inner, after)
    restrict, expand = transfer_matrices()
    fine = lambda n, r: pltpu.VMEM((n, 2, r, 128), F32)
    coarse = lambda n: pltpu.VMEM((16 * n, 128), F32)
    out = jax.ShapeDtypeStruct((2, L, 8, 128), F32)
    return pl.pallas_call(
        main_kernel,
        out_shape=(out, out),
        in_specs=[smem] + [vmem] * 7,
        out_specs=(vmem, vmem),
        scratch_shapes=[
            fine(40, 56), fine(5, 40), fine(20, 48), fine(20, 32), fine(20, 32), fine(20, 32), fine(40, 32), fine(40, 32),
            fine(40, 32), fine(40, 32), fine(40, 40), fine(40, 48),
            pltpu.VMEM((2, 63 * 16, 128), F32), coarse(63), pltpu.VMEM((320, 128), F32), pltpu.VMEM((2, 320, 128), F32),
            coarse(41), coarse(21), coarse(20), coarse(40), coarse(40), coarse(40), fine(40, 16),
        ],
        compiler_params=pltpu.CompilerParams(vmem_limit_bytes=48 * 1024 * 1024),
        name="cycle",
    )(*parts, restrict, expand)


def solution(mesh):
    return jax.shard_map(
        per_device,
        mesh=mesh,
        in_specs=(
            P(None, None, "gx", "gy"),
            P(None, "gx", "gy"),
            P("gx", "gy"),
            P("gx", "gy"),
            P("gx", "gy"),
            P("gx", "gy"),
            P(),
        ),
        out_specs=(P(None, None, "gx", "gy"), P(None, None, "gx", "gy")),
        check_vma=False,
    )
```

time: 44.8 us -> 44 us (0.982)
  Pallas kernels: 11.8 us -> 10.9 us
    pallas_call x1, Pallas kernels: 10.1 us -> 9.24 us  [per_device(): pl.pallas_call(main_kernel, out_shape=(out, out), in_specs=[smem] + [vmem...]
where the time goes in v4:
time: 44 us; the launch traced here: 43.7 us
  starting transfers between devices  20 us (45%)
  waiting for transfers between devices  11.8 us (27%)
  Pallas kernels  10.9 us (25%)
  between operations  0.78 us (2%)
    ppermute x6, starting transfers between devices, send(): return lax.ppermute(cells, ('gx', 'gy'), pairs(move)(axis))  20 us
    ppermute x6, waiting for transfers between devices, send(): return lax.ppermute(cells, ('gx', 'gy'), pairs(move)(axis))  11.8 us
    pallas_call x1, Pallas kernels, per_device(): pl.pallas_call(main_kernel, out_shape=(out, out), in_specs=[smem] + [vmem...  9.24 us
    pallas_call x1, Pallas kernels, per_device(): pl.pallas_call(pack_kernel, out_shape=(jax.ShapeDtypeStruct((PLANES, 8, 1...  1.71 us
  transfers between devices with their start and end apart: 6, of which 3 were waited for; matrix products, arithmetic and copies ran while one was open for 0% of the time, Pallas kernels for 0%

profile of v4, /device:TPU:408, one launch (start us, length us, event | category | flops | bytes accessed | tf_op | source)
XLA Modules:
  0.0 43.7 jit_solution(8134035838533061571)
XLA Ops:
  0.6 1.7 %pack.1 = (f32[45,8,128]{2,1,0:T(8,128)}, f32[12,8,128]{2,1,0:T(8,128)}) custom-call(f32[2,20,8,128]{3,2,1,0:T(8,128)} %vel.1, f32[2,8,128]{2,1,0:T(8,128)} %drive.1, f32[8,128]{1,0:T(8,128)} %stiff.1, f32[8,128]{1,0:T(8,128)} %thick.1, s32[8,128]{1,0:T(8,128)} %ice.1, s32[8,128]{1,0:T(8,128)} %cls.1, f32[8]{0:T(128)} %table.1), custom_call_target="tpu_custom_call" | custom-call | tf_op jit(solution)/shard_map/pack/pallas_call | solution.py:444
  2.3 0.0 copy-start
  2.3 4.4 %collective-permute-start.1 = (f32[12,8,128]{2,1,0:T(8,128)}, f32[12,8,128]{2,1,0:T(8,128)S(1)}, u32[]{:S(2)}, u32[]{:S(2)}) collective-permute-start(f32[12,8,128]{2,1,0:T(8,128)} %get-tuple-element.5), channel_id=1, source_target_pairs={{1,2},{2,1},{3,4},{4,3},{5,6},{6,5},{7,8},{8,7},{9,10},{10,9},{11,... | collective-permute-start | bytes 147464 | tf_op jit(solution)/shard_map/ppermute | solution.py:430
  6.8 1.9 %collective-permute-start = (f32[12,8,128]{2,1,0:T(8,128)}, f32[12,8,128]{2,1,0:T(8,128)S(1)}, u32[]{:S(2)}, u32[]{:S(2)}) collective-permute-start(f32[12,8,128]{2,1,0:T(8,128)} %get-tuple-element.5), channel_id=1, source_target_pairs={{0,1},{1,0},{2,3},{3,2},{4,5},{5,4},{6,7},{7,6},{8,9},{9,8},{10,11... | collective-permute-start | bytes 147464 | tf_op jit(solution)/shard_map/ppermute | solution.py:430
  8.8 1.4 %collective-permute-done.1 = f32[12,8,128]{2,1,0:T(8,128)S(1)} collective-permute-done((f32[12,8,128]{2,1,0:T(8,128)}, f32[12,8,128]{2,1,0:T(8,128)S(1)}, u32[]{:S(2)}, u32[]{:S(2)}) %collective-permute-start.1) | collective-permute-done | bytes 49184 | tf_op jit(solution)/shard_map/ppermute | solution.py:430
  10.2 0.0 collective-permute-done
  10.2 0.0 copy-done
  10.2 4.1 %collective-permute-start.5 = (f32[57,8,128]{2,1,0:T(8,128)S(1)}, f32[57,8,128]{2,1,0:T(8,128)S(1)}, u32[]{:S(2)}, u32[]{:S(2)}) collective-permute-start(f32[57,8,128]{2,1,0:T(8,128)S(1)} %pad_maximum_fusion.g0), channel_id=1, source_target_pairs={{32,0},{33,1},{34,2},{35,3},{36,4},{37,5},{38,6},{39,7},{40,8},{41... | collective-permute-start | bytes 700424 | tf_op jit(solution)/shard_map/ppermute | solution.py:430
  14.4 3.1 %collective-permute-start.4 = (f32[57,8,128]{2,1,0:T(8,128)S(1)}, f32[57,8,128]{2,1,0:T(8,128)S(1)}, u32[]{:S(2)}, u32[]{:S(2)}) collective-permute-start(f32[57,8,128]{2,1,0:T(8,128)S(1)} %pad_maximum_fusion.g0), channel_id=1, source_target_pairs={{0,16},{1,17},{2,18},{3,19},{4,20},{5,21},{6,22},{7,23},{8,24},{9,... | collective-permute-start | bytes 700424 | tf_op jit(solution)/shard_map/ppermute | solution.py:430
  17.5 3.4 %collective-permute-start.3 = (f32[57,8,128]{2,1,0:T(8,128)S(1)}, f32[57,8,128]{2,1,0:T(8,128)S(1)}, u32[]{:S(2)}, u32[]{:S(2)}) collective-permute-start(f32[57,8,128]{2,1,0:T(8,128)S(1)} %pad_maximum_fusion.g0), channel_id=1, source_target_pairs={{16,32},{17,33},{18,34},{19,35},{20,36},{21,37},{22,38},{23,39},{2... | collective-permute-start | bytes 700424 | tf_op jit(solution)/shard_map/ppermute | solution.py:430
  21.0 2.9 %collective-permute-start.2 = (f32[57,8,128]{2,1,0:T(8,128)S(1)}, f32[57,8,128]{2,1,0:T(8,128)S(1)}, u32[]{:S(2)}, u32[]{:S(2)}) collective-permute-start(f32[57,8,128]{2,1,0:T(8,128)S(1)} %pad_maximum_fusion.g0), channel_id=1, source_target_pairs={{0,32},{1,33},{2,34},{3,35},{4,36},{5,37},{6,38},{7,39},{8,40},{9,... | collective-permute-start | bytes 700424 | tf_op jit(solution)/shard_map/ppermute | solution.py:430
  23.9 0.1 select_convert_fusion
  24.1 0.0 collective-permute-done.5.gp2
  24.1 6.1 %collective-permute-done.4.swap_a = f32[57,8,128]{2,1,0:T(8,128)S(1)} collective-permute-done((f32[57,8,128]{2,1,0:T(8,128)S(1)}, f32[57,8,128]{2,1,0:T(8,128)S(1)}, u32[]{:S(2)}, u32[]{:S(2)}) %collective-permute-start.4) | collective-permute-done | bytes 233504 | tf_op jit(solution)/shard_map/ppermute | solution.py:430
  30.2 0.0 collective-permute-done.3.swap_b
  30.2 4.3 %collective-permute-done.2.gm2 = f32[57,8,128]{2,1,0:T(8,128)S(1)} collective-permute-done((f32[57,8,128]{2,1,0:T(8,128)S(1)}, f32[57,8,128]{2,1,0:T(8,128)S(1)}, u32[]{:S(2)}, u32[]{:S(2)}) %collective-permute-start.2) | collective-permute-done | bytes 233504 | tf_op jit(solution)/shard_map/ppermute | solution.py:430
  34.5 9.2 %cycle.1 = (f32[2,20,8,128]{3,2,1,0:T(8,128)}, f32[2,20,8,128]{3,2,1,0:T(8,128)}) custom-call(s32[1]{0:T(128)} %bitcast.parity, f32[57,8,128]{2,1,0:T(8,128)S(1)} %collective-permute-done.2.gm2, f32[57,8,128]{2,1,0:T(8,128)S(1)} %collective-permute-done.3.swap_b, f32[57,8,128]{2,1,0:T(8,128)S(1)} %pad_maximum_fusion.g0, ...), custom_call_target="tpu_custom_call" | custom-call | tf_op jit(solution)/shard_map/cycle/pallas_call | solution.py:469
  (8 shorter events, 0.1 us)
Async XLA Ops:
  2.3 7.9 %copy-start = (f32[45,8,128]{2,1,0:T(8,128)S(1)}, f32[45,8,128]{2,1,0:T(8,128)}, u32[]{:S(2)}) copy-start(f32[45,8,128]{2,1,0:T(8,128)} %get-tuple-element.4) | copy-start | bytes 552964
  2.3 7.8 %collective-permute-start.1 = (f32[12,8,128]{2,1,0:T(8,128)}, f32[12,8,128]{2,1,0:T(8,128)S(1)}, u32[]{:S(2)}, u32[]{:S(2)}) collective-permute-start(f32[12,8,128]{2,1,0:T(8,128)} %get-tuple-element.5), channel_id=1, source_target_pairs={{1,2},{2,1},{3,4},{4,3},{5,6},{6,5},{7,8},{8,7},{9,10},{10,9},{11,... | collective-permute-start | bytes 147464 | tf_op jit(solution)/shard_map/ppermute | solution.py:430
  6.8 3.4 %collective-permute-start = (f32[12,8,128]{2,1,0:T(8,128)}, f32[12,8,128]{2,1,0:T(8,128)S(1)}, u32[]{:S(2)}, u32[]{:S(2)}) collective-permute-start(f32[12,8,128]{2,1,0:T(8,128)} %get-tuple-element.5), channel_id=1, source_target_pairs={{0,1},{1,0},{2,3},{3,2},{4,5},{5,4},{6,7},{7,6},{8,9},{9,8},{10,11... | collective-permute-start | bytes 147464 | tf_op jit(solution)/shard_map/ppermute | solution.py:430
  10.2 13.8 %collective-permute-start.5 = (f32[57,8,128]{2,1,0:T(8,128)S(1)}, f32[57,8,128]{2,1,0:T(8,128)S(1)}, u32[]{:S(2)}, u32[]{:S(2)}) collective-permute-start(f32[57,8,128]{2,1,0:T(8,128)S(1)} %pad_maximum_fusion.g0), channel_id=1, source_target_pairs={{32,0},{33,1},{34,2},{35,3},{36,4},{37,5},{38,6},{39,7},{40,8},{41... | collective-permute-start | bytes 700424 | tf_op jit(solution)/shard_map/ppermute | solution.py:430
  14.4 15.8 %collective-permute-start.4 = (f32[57,8,128]{2,1,0:T(8,128)S(1)}, f32[57,8,128]{2,1,0:T(8,128)S(1)}, u32[]{:S(2)}, u32[]{:S(2)}) collective-permute-start(f32[57,8,128]{2,1,0:T(8,128)S(1)} %pad_maximum_fusion.g0), channel_id=1, source_target_pairs={{0,16},{1,17},{2,18},{3,19},{4,20},{5,21},{6,22},{7,23},{8,24},{9,... | collective-permute-start | bytes 700424 | tf_op jit(solution)/shard_map/ppermute | solution.py:430
  17.5 12.6 %collective-permute-start.3 = (f32[57,8,128]{2,1,0:T(8,128)S(1)}, f32[57,8,128]{2,1,0:T(8,128)S(1)}, u32[]{:S(2)}, u32[]{:S(2)}) collective-permute-start(f32[57,8,128]{2,1,0:T(8,128)S(1)} %pad_maximum_fusion.g0), channel_id=1, source_target_pairs={{16,32},{17,33},{18,34},{19,35},{20,36},{21,37},{22,38},{23,39},{2... | collective-permute-start | bytes 700424 | tf_op jit(solution)/shard_map/ppermute | solution.py:430
  21.0 13.5 %collective-permute-start.2 = (f32[57,8,128]{2,1,0:T(8,128)S(1)}, f32[57,8,128]{2,1,0:T(8,128)S(1)}, u32[]{:S(2)}, u32[]{:S(2)}) collective-permute-start(f32[57,8,128]{2,1,0:T(8,128)S(1)} %pad_maximum_fusion.g0), channel_id=1, source_target_pairs={{0,32},{1,33},{2,34},{3,35},{4,36},{5,37},{6,38},{7,39},{8,40},{9,... | collective-permute-start | bytes 700424 | tf_op jit(solution)/shard_map/ppermute | solution.py:430

commit v5 on v4

--- a/solution.py
+++ b/solution.py
@@ -125,7 +125,7 @@
         uy = [[uc[lt][k][1] - uc[lt][k][0] for k in range(5)] for lt in range(2)]
         v, vr, vc = around(V, z + L, range(5))
         for lt in range(2):
-            for k in range(5):
+            for k in range(5 - lt):
                 vx = vr[lt][k][1] - vr[lt][k][0]
                 vy = vc[lt][k][1] - vc[lt][k][0]
                 uz = V[after, lt, inside(k), :] - V[before, lt, inside(k), :]
@@ -149,6 +149,10 @@
         return 0
 
     lax.fori_loop(0, L, visc, 0, unroll=UNROLL)
+    for z in range(L):
+        for place in (slice(0, 8), slice(40, 48)):
+            for ref, p in ((Q, z), (X, z), (X, z + L)):
+                ref[p, 1, place, :] = jnp.zeros((8, 128), F32)
 
     def factor(z, carry):
         top = jnp.where(z < L - 1, 1.0, 0.0)
@@ -262,7 +266,7 @@
             CA[lt, pl.ds(pl.multiple_of(p * 16, 16), 16), :] = T[p, lt, even, :] + T[p, lt, odd, :]
         return 0
 
-    lax.fori_loop(0, 40, gather, 0, unroll=UNROLL)
+    lax.fori_loop(0, 40, gather, 0, unroll=40)
 
     def gather_eta(z, _):
         for lt in range(2):
@@ -373,7 +377,7 @@
         )
         return 0
 
-    lax.fori_loop(0, 40, spread, 0, unroll=UNROLL)
+    lax.fori_loop(0, 40, spread, 0, unroll=40)
     for lt in range(2):
         CF[lt] = product(CE[...], expand[lt])
 
@@ -387,7 +391,7 @@
                 X[p, lt, inside(k), :] = X[p, lt, inside(k), :] + q * PC[p, lt, rows(k - 1), :]
         return 0
 
-    lax.fori_loop(0, 40, correct, 0, unroll=UNROLL)
+    lax.fori_loop(0, 40, correct, 0, unroll=40)
 
     post = [1, 2]
     for _ in range(2):
@@ -458,8 +462,8 @@
     whole = jnp.concatenate([main, rim], axis=0)
     before = send(whole, "gx", lambda i: i + 2)
     after = send(whole, "gx", lambda i: i - 2)
+    inner = send(whole, "gx", inner_swap)
     outer = send(whole, "gx", outer_swap)
-    inner = send(whole, "gx", inner_swap)
     parity = (lax.axis_index("gx") % 2).astype(jnp.int32).reshape(1)
     parts = (parity, before, outer, whole, inner, after)
     restrict, expand = transfer_matrices()

time: 44 us -> 43.8 us (level)
  no operation moved by 1% of the time
where the time goes in v5:
time: 43.8 us; the launch traced here: 43.6 us
  starting transfers between devices  20 us (46%)
  waiting for transfers between devices  11.8 us (27%)
  Pallas kernels  10.8 us (25%)
  between operations  0.78 us (2%)
    ppermute x6, starting transfers between devices, send(): return lax.ppermute(cells, ('gx', 'gy'), pairs(move)(axis))  20 us
    ppermute x6, waiting for transfers between devices, send(): return lax.ppermute(cells, ('gx', 'gy'), pairs(move)(axis))  11.8 us
    pallas_call x1, Pallas kernels, per_device(): pl.pallas_call(main_kernel, out_shape=(out, out), in_specs=[smem] + [vmem...  9.11 us
    pallas_call x1, Pallas kernels, per_device(): pl.pallas_call(pack_kernel, out_shape=(jax.ShapeDtypeStruct((PLANES, 8, 1...  1.71 us
  transfers between devices with their start and end apart: 6, of which 3 were waited for; matrix products, arithmetic and copies ran while one was open for 0% of the time, Pallas kernels for 0%

profile of v5, /device:TPU:408, one launch (start us, length us, event | category | flops | bytes accessed | tf_op | source)
XLA Modules:
  0.0 43.6 jit_solution(16653721910752470917)
XLA Ops:
  0.6 1.7 %pack.1 = (f32[45,8,128]{2,1,0:T(8,128)}, f32[12,8,128]{2,1,0:T(8,128)}) custom-call(f32[2,20,8,128]{3,2,1,0:T(8,128)} %vel.1, f32[2,8,128]{2,1,0:T(8,128)} %drive.1, f32[8,128]{1,0:T(8,128)} %stiff.1, f32[8,128]{1,0:T(8,128)} %thick.1, s32[8,128]{1,0:T(8,128)} %ice.1, s32[8,128]{1,0:T(8,128)} %cls.1, f32[8]{0:T(128)} %table.1), custom_call_target="tpu_custom_call" | custom-call | tf_op jit(solution)/shard_map/pack/pallas_call | solution.py:448
  2.3 0.0 copy-start
  2.3 4.4 %collective-permute-start.1 = (f32[12,8,128]{2,1,0:T(8,128)}, f32[12,8,128]{2,1,0:T(8,128)S(1)}, u32[]{:S(2)}, u32[]{:S(2)}) collective-permute-start(f32[12,8,128]{2,1,0:T(8,128)} %get-tuple-element.5), channel_id=1, source_target_pairs={{1,2},{2,1},{3,4},{4,3},{5,6},{6,5},{7,8},{8,7},{9,10},{10,9},{11,... | collective-permute-start | bytes 147464 | tf_op jit(solution)/shard_map/ppermute | solution.py:434
  6.8 1.9 %collective-permute-start = (f32[12,8,128]{2,1,0:T(8,128)}, f32[12,8,128]{2,1,0:T(8,128)S(1)}, u32[]{:S(2)}, u32[]{:S(2)}) collective-permute-start(f32[12,8,128]{2,1,0:T(8,128)} %get-tuple-element.5), channel_id=1, source_target_pairs={{0,1},{1,0},{2,3},{3,2},{4,5},{5,4},{6,7},{7,6},{8,9},{9,8},{10,11... | collective-permute-start | bytes 147464 | tf_op jit(solution)/shard_map/ppermute | solution.py:434
  8.8 1.4 %collective-permute-done.1 = f32[12,8,128]{2,1,0:T(8,128)S(1)} collective-permute-done((f32[12,8,128]{2,1,0:T(8,128)}, f32[12,8,128]{2,1,0:T(8,128)S(1)}, u32[]{:S(2)}, u32[]{:S(2)}) %collective-permute-start.1) | collective-permute-done | bytes 49184 | tf_op jit(solution)/shard_map/ppermute | solution.py:434
  10.2 0.0 collective-permute-done
  10.2 0.0 copy-done
  10.2 4.1 %collective-permute-start.5 = (f32[57,8,128]{2,1,0:T(8,128)S(1)}, f32[57,8,128]{2,1,0:T(8,128)S(1)}, u32[]{:S(2)}, u32[]{:S(2)}) collective-permute-start(f32[57,8,128]{2,1,0:T(8,128)S(1)} %pad_maximum_fusion.g0), channel_id=1, source_target_pairs={{32,0},{33,1},{34,2},{35,3},{36,4},{37,5},{38,6},{39,7},{40,8},{41... | collective-permute-start | bytes 700424 | tf_op jit(solution)/shard_map/ppermute | solution.py:434
  14.4 3.1 %collective-permute-start.4 = (f32[57,8,128]{2,1,0:T(8,128)S(1)}, f32[57,8,128]{2,1,0:T(8,128)S(1)}, u32[]{:S(2)}, u32[]{:S(2)}) collective-permute-start(f32[57,8,128]{2,1,0:T(8,128)S(1)} %pad_maximum_fusion.g0), channel_id=1, source_target_pairs={{0,16},{1,17},{2,18},{3,19},{4,20},{5,21},{6,22},{7,23},{8,24},{9,... | collective-permute-start | bytes 700424 | tf_op jit(solution)/shard_map/ppermute | solution.py:434
  17.5 3.4 %collective-permute-start.3 = (f32[57,8,128]{2,1,0:T(8,128)S(1)}, f32[57,8,128]{2,1,0:T(8,128)S(1)}, u32[]{:S(2)}, u32[]{:S(2)}) collective-permute-start(f32[57,8,128]{2,1,0:T(8,128)S(1)} %pad_maximum_fusion.g0), channel_id=1, source_target_pairs={{16,32},{17,33},{18,34},{19,35},{20,36},{21,37},{22,38},{23,39},{2... | collective-permute-start | bytes 700424 | tf_op jit(solution)/shard_map/ppermute | solution.py:434
  21.0 2.9 %collective-permute-start.2 = (f32[57,8,128]{2,1,0:T(8,128)S(1)}, f32[57,8,128]{2,1,0:T(8,128)S(1)}, u32[]{:S(2)}, u32[]{:S(2)}) collective-permute-start(f32[57,8,128]{2,1,0:T(8,128)S(1)} %pad_maximum_fusion.g0), channel_id=1, source_target_pairs={{0,32},{1,33},{2,34},{3,35},{4,36},{5,37},{6,38},{7,39},{8,40},{9,... | collective-permute-start | bytes 700424 | tf_op jit(solution)/shard_map/ppermute | solution.py:434
  23.9 0.1 select_convert_fusion
  24.1 0.0 collective-permute-done.5.gp2
  24.1 6.1 %collective-permute-done.4.swap_a = f32[57,8,128]{2,1,0:T(8,128)S(1)} collective-permute-done((f32[57,8,128]{2,1,0:T(8,128)S(1)}, f32[57,8,128]{2,1,0:T(8,128)S(1)}, u32[]{:S(2)}, u32[]{:S(2)}) %collective-permute-start.4) | collective-permute-done | bytes 233504 | tf_op jit(solution)/shard_map/ppermute | solution.py:434
  30.2 0.0 collective-permute-done.3.swap_b
  30.2 4.3 %collective-permute-done.2.gm2 = f32[57,8,128]{2,1,0:T(8,128)S(1)} collective-permute-done((f32[57,8,128]{2,1,0:T(8,128)S(1)}, f32[57,8,128]{2,1,0:T(8,128)S(1)}, u32[]{:S(2)}, u32[]{:S(2)}) %collective-permute-start.2) | collective-permute-done | bytes 233504 | tf_op jit(solution)/shard_map/ppermute | solution.py:434
  34.5 9.1 %cycle.1 = (f32[2,20,8,128]{3,2,1,0:T(8,128)}, f32[2,20,8,128]{3,2,1,0:T(8,128)}) custom-call(s32[1]{0:T(128)} %bitcast.parity, f32[57,8,128]{2,1,0:T(8,128)S(1)} %collective-permute-done.2.gm2, f32[57,8,128]{2,1,0:T(8,128)S(1)} %collective-permute-done.3.swap_b, f32[57,8,128]{2,1,0:T(8,128)S(1)} %pad_maximum_fusion.g0, ...), custom_call_target="tpu_custom_call" | custom-call | tf_op jit(solution)/shard_map/cycle/pallas_call | solution.py:473
  (8 shorter events, 0.1 us)
Async XLA Ops:
  2.3 7.9 %copy-start = (f32[45,8,128]{2,1,0:T(8,128)S(1)}, f32[45,8,128]{2,1,0:T(8,128)}, u32[]{:S(2)}) copy-start(f32[45,8,128]{2,1,0:T(8,128)} %get-tuple-element.4) | copy-start | bytes 552964
  2.3 7.8 %collective-permute-start.1 = (f32[12,8,128]{2,1,0:T(8,128)}, f32[12,8,128]{2,1,0:T(8,128)S(1)}, u32[]{:S(2)}, u32[]{:S(2)}) collective-permute-start(f32[12,8,128]{2,1,0:T(8,128)} %get-tuple-element.5), channel_id=1, source_target_pairs={{1,2},{2,1},{3,4},{4,3},{5,6},{6,5},{7,8},{8,7},{9,10},{10,9},{11,... | collective-permute-start | bytes 147464 | tf_op jit(solution)/shard_map/ppermute | solution.py:434
  6.8 3.4 %collective-permute-start = (f32[12,8,128]{2,1,0:T(8,128)}, f32[12,8,128]{2,1,0:T(8,128)S(1)}, u32[]{:S(2)}, u32[]{:S(2)}) collective-permute-start(f32[12,8,128]{2,1,0:T(8,128)} %get-tuple-element.5), channel_id=1, source_target_pairs={{0,1},{1,0},{2,3},{3,2},{4,5},{5,4},{6,7},{7,6},{8,9},{9,8},{10,11... | collective-permute-start | bytes 147464 | tf_op jit(solution)/shard_map/ppermute | solution.py:434
  10.2 13.8 %collective-permute-start.5 = (f32[57,8,128]{2,1,0:T(8,128)S(1)}, f32[57,8,128]{2,1,0:T(8,128)S(1)}, u32[]{:S(2)}, u32[]{:S(2)}) collective-permute-start(f32[57,8,128]{2,1,0:T(8,128)S(1)} %pad_maximum_fusion.g0), channel_id=1, source_target_pairs={{32,0},{33,1},{34,2},{35,3},{36,4},{37,5},{38,6},{39,7},{40,8},{41... | collective-permute-start | bytes 700424 | tf_op jit(solution)/shard_map/ppermute | solution.py:434
  14.4 15.8 %collective-permute-start.4 = (f32[57,8,128]{2,1,0:T(8,128)S(1)}, f32[57,8,128]{2,1,0:T(8,128)S(1)}, u32[]{:S(2)}, u32[]{:S(2)}) collective-permute-start(f32[57,8,128]{2,1,0:T(8,128)S(1)} %pad_maximum_fusion.g0), channel_id=1, source_target_pairs={{0,16},{1,17},{2,18},{3,19},{4,20},{5,21},{6,22},{7,23},{8,24},{9,... | collective-permute-start | bytes 700424 | tf_op jit(solution)/shard_map/ppermute | solution.py:434
  17.5 12.6 %collective-permute-start.3 = (f32[57,8,128]{2,1,0:T(8,128)S(1)}, f32[57,8,128]{2,1,0:T(8,128)S(1)}, u32[]{:S(2)}, u32[]{:S(2)}) collective-permute-start(f32[57,8,128]{2,1,0:T(8,128)S(1)} %pad_maximum_fusion.g0), channel_id=1, source_target_pairs={{16,32},{17,33},{18,34},{19,35},{20,36},{21,37},{22,38},{23,39},{2... | collective-permute-start | bytes 700424 | tf_op jit(solution)/shard_map/ppermute | solution.py:434
  21.0 13.5 %collective-permute-start.2 = (f32[57,8,128]{2,1,0:T(8,128)S(1)}, f32[57,8,128]{2,1,0:T(8,128)S(1)}, u32[]{:S(2)}, u32[]{:S(2)}) collective-permute-start(f32[57,8,128]{2,1,0:T(8,128)S(1)} %pad_maximum_fusion.g0), channel_id=1, source_target_pairs={{0,32},{1,33},{2,34},{3,35},{4,36},{5,37},{6,38},{7,39},{8,40},{9,... | collective-permute-start | bytes 700424 | tf_op jit(solution)/shard_map/ppermute | solution.py:434
